TPU v7x, 128 devices: a whole 4x4x4 slice. The times are simulated.
128 devices in a mesh: grp: 4 (over z), chan: 32 (over x, y, core).
Axes of the slice: x: 4, y: 4, z: 4, core: 2. Of those that a mesh axis runs over, the one named last changes fastest.
Arguments:
- jones_start: float32 [256, 8, 64, 62], P(('grp', 'chan')), may hold values from -0.9 to 1.9
- duals_start: float32 [256, 8, 64, 62], P(('grp', 'chan')), may hold values from -2.5 to 2.5
- consensus_start: float32 [3, 8, 64, 62], replicated, may hold values from -0.6 to 1.6
- visibilities: float32 [256, 8, 1891], P(('grp', 'chan')), may hold values from -6 to 6
- coherencies: bfloat16 [256, 8, 64, 1891], P(('grp', 'chan')), may hold values from -0.59765625 to 0.59765625
- pairs: int32 [2, 1891], replicated, may hold values from 0 to 61, as said below
- counts: int32 [256], P(('grp', 'chan')), may hold values from 1 to 16
Outputs:
- jones: float32 [256, 8, 64, 62], P(('grp', 'chan'))
- duals: float32 [256, 8, 64, 62], P(('grp', 'chan'))
- consensus: float32 [3, 8, 64, 62], replicated
Inputs may be any that keep to these rules, and one draw needn't show every extreme that they name: `pairs`: row 0 and row 1 name the two stations of a baseline; every unordered pair of distinct stations appears exactly once, in either order.
All inputs are finite; a program needn't handle non-finite values.
Results may differ from a plain program's by a relative error of at most 0.0003.
Values sent between devices are 32-bit elements; how exact they have to be, the bound alone decides.
A program may use at most 128 MiB of HBM per device.

v0:
```python
import jax
import jax.numpy as jnp
from jax import lax
from jax.sharding import PartitionSpec as P

SAMPLES = 16
STEPS = 2


ETA_STEP = 0.08
RHO_PENALTY = 1.0
HIGHEST_PRECISION = lax.Precision.HIGHEST


def as_complex(stacked):
    return [
        (stacked[0], stacked[1]),
        (stacked[2], stacked[3]),
        (stacked[4], stacked[5]),
        (stacked[6], stacked[7]),
    ]


def as_stacked(matrix):
    return jnp.stack([component for element in matrix for component in element])


def complex_product(former, latter):
    return (
        former[0] * latter[0] - former[1] * latter[1],
        former[0] * latter[1] + former[1] * latter[0],
    )


def complex_sum(former, latter):
    return (former[0] + latter[0], former[1] + latter[1])


def matrix_product(former, latter):
    upper_left = complex_sum(
        complex_product(former[0], latter[0]), complex_product(former[1], latter[2])
    )
    upper_right = complex_sum(
        complex_product(former[0], latter[1]), complex_product(former[1], latter[3])
    )
    lower_left = complex_sum(
        complex_product(former[2], latter[0]), complex_product(former[3], latter[2])
    )
    lower_right = complex_sum(
        complex_product(former[2], latter[1]), complex_product(former[3], latter[3])
    )
    return [upper_left, upper_right, lower_left, lower_right]


def conjugate(element):
    return (element[0], -element[1])


def adjoint(matrix):
    return [conjugate(matrix[0]), conjugate(matrix[2]), conjugate(matrix[1]), conjugate(matrix[3])]


def data_gradient(first_jones, second_jones, coherency, observed, weight):
    first_terms = as_complex(first_jones)
    second_terms = as_complex(second_jones)
    source_terms = as_complex(coherency.astype(jnp.float32))
    propagated = matrix_product(first_terms, source_terms)
    predicted = jnp.sum(as_stacked(matrix_product(propagated, adjoint(second_terms))), axis=1)
    residual = as_complex((observed - predicted)[:, None, :])
    conjugated = matrix_product(second_terms, adjoint(source_terms))
    factor = -2.0 * weight
    grad_first = factor * as_stacked(matrix_product(residual, conjugated))
    grad_second = factor * as_stacked(matrix_product(adjoint(residual), propagated))
    return (grad_first, grad_second)


def bernstein(position):
    return jnp.stack(
        [
            (1.0 - position) * (1.0 - position),
            2.0 * position * (1.0 - position),
            position * position,
        ]
    )


def inverse_three(matrix):
    cross_rows = jnp.stack(
        [
            jnp.cross(matrix[1], matrix[2]),
            jnp.cross(matrix[2], matrix[0]),
            jnp.cross(matrix[0], matrix[1]),
        ]
    )
    determinant = jnp.sum(matrix[0] * cross_rows[0])
    return cross_rows.T / determinant


def gram_inverse(channels):
    position = (jnp.arange(channels, dtype=jnp.float32) + 0.5) / channels
    values = bernstein(position)
    return inverse_three(jnp.dot(values, values.T, precision=HIGHEST_PRECISION))


def descend(jones, duals, target, coherency, observed, weight, collect, spread):
    for step_index in range(STEPS):
        first_jones, second_jones = collect(jones)
        grad_first, grad_second = data_gradient(
            first_jones, second_jones, coherency, observed, weight
        )
        gradient = spread(grad_first, grad_second) + RHO_PENALTY * (jones - target) + duals
        jones = jones - ETA_STEP * gradient
    return jones


def shards(jones_start, duals_start, consensus_start, visibilities, coherencies, pairs, counts):
    chan_local = jones_start.shape[0]
    stations = jones_start.shape[3]
    blocks = lax.axis_size("chan")
    channels = chan_local * lax.axis_size("grp") * blocks
    offset = (lax.axis_index("grp") * blocks + lax.axis_index("chan")) * chan_local
    inverse = gram_inverse(channels)
    own_index = offset + jnp.arange(chan_local, dtype=jnp.int32)
    basis_values = bernstein((own_index.astype(jnp.float32) + 0.5) / channels)
    weights = counts.astype(jnp.float32) / SAMPLES
    station_ids = jnp.arange(stations, dtype=jnp.int32)[:, None]
    first_table = (pairs[0][None, :] == station_ids).astype(jnp.float32)
    second_table = (pairs[1][None, :] == station_ids).astype(jnp.float32)
    both_tables = jnp.concatenate([first_table, second_table], axis=1)

    def collect(jones):
        first_jones = jnp.einsum("kds,sb->kdb", jones, first_table, precision=HIGHEST_PRECISION)
        second_jones = jnp.einsum("kds,sb->kdb", jones, second_table, precision=HIGHEST_PRECISION)
        return (first_jones, second_jones)

    def spread(grad_first, grad_second):
        joined = jnp.concatenate([grad_first, grad_second], axis=2)
        return jnp.einsum("kdb,sb->kds", joined, both_tables, precision=HIGHEST_PRECISION)

    jones, duals, consensus = (jones_start, duals_start, consensus_start)

    def update(packed):
        local_jones, local_duals, coherency, observed, weight, column = packed
        target = jnp.einsum("i,ikds->kds", column, consensus, precision=HIGHEST_PRECISION)
        return descend(
            local_jones, local_duals, target, coherency, observed, weight, collect, spread
        )

    jones = lax.map(update, (jones, duals, coherencies, visibilities, weights, basis_values.T))
    local_sums = jnp.einsum(
        "ic,ckds->ikds", basis_values, jones + duals / RHO_PENALTY, precision=HIGHEST_PRECISION
    )
    group_sums = lax.psum(local_sums, "chan")
    sums = lax.psum(group_sums, "grp")
    consensus = jnp.einsum("ij,jkds->ikds", inverse, sums, precision=HIGHEST_PRECISION)
    smooth = jnp.einsum("ic,ikds->ckds", basis_values, consensus, precision=HIGHEST_PRECISION)
    duals = duals + RHO_PENALTY * (jones - smooth)
    return (jones, duals, consensus)


def solution(mesh):
    in_specs = (
        P(("grp", "chan"), None, None, None),
        P(("grp", "chan"), None, None, None),
        P(),
        P(("grp", "chan"), None, None),
        P(("grp", "chan"), None, None, None),
        P(),
        P(("grp", "chan")),
    )
    out_specs = (P(("grp", "chan"), None, None, None), P(("grp", "chan"), None, None, None), P())
    return jax.shard_map(shards, mesh=mesh, in_specs=in_specs, out_specs=out_specs, check_vma=False)
```

profile of v0, /device:TPU:1, one launch (start us, length us, event | category | flops | bytes accessed | tf_op | source)
XLA Modules:
  0.0 360.0 jit_solution(14905752037207974579)
XLA Ops:
  12.2 172.9 %while.11 = (s32[]{:T(128)}, f32[2,8,64,62]{3,2,1,0:T(8,128)}, f32[2,8,64,62]{2,1,3,0:T(8,128)}, f32[2]{0:T(128)S(1)}, f32[2,8,1891]{2,1,0:T(8,128)}, /*index=5*...) while((s32[]{:T(128)}, f32[2,8,64,62]{3,2,1,0:T(8,128)}, ...), condition=%wide.region_3.4_spmd.clone, body=%wide.region_0.3_spmd.clone.sunk | while | flops 5848357376 | bytes 441545632 | solution.py:149
  13.6 3.3 fusion.137
  17.3 3.3 fusion.138
  29.7 2.4 reduce_sum.33
  33.3 3.4 add_dynamic-update-slice_fusion.102
  49.8 9.5 %fusion.140 = f32[8,64,62]{2,1,0:T(8,128)S(1)} fusion(f32[8,64,1891]{2,1,0:T(8,128)} %broadcast_multiply_fusion.7, f32[8,64,1891]{2,1,0:T(8,128)} %broadcast_multiply_fusion.8, f32[62,3782]{1,0:T(8,128)S(1)} %copy-done.12, f32[1,8,64,62]{3,2,1,0:T(8,128)S(1)} %copy.36, f32[1,8,64,62]{3,2,1,0:T(8,128)S(1)} %copy-done.17, ...), kind=kOutput, calls=%fused_computation.24.clone.1 | convolution fusion | flops 1442764800 | bytes 9191380 | tf_op jit(solution)/shard_map/while/body/eval_jaxpr/kdb,sb->kds/dot_general | solution.py:138
  59.3 3.3 fusion.141
  62.7 3.3 fusion.142
  75.1 2.4 reduce_sum.34
  78.7 3.4 add_dynamic-update-slice_fusion.125
  88.6 6.3 %fusion.143 = f32[2,8,64,62]{3,2,1,0:T(8,128)S(1)} fusion(f32[2,8,64,62]{3,2,1,0:T(8,128)S(1)} %copy-done.24, s32[]{:T(128)S(6)} %copy.82, f32[8,64,62]{2,1,0:T(8,128)S(1)} %copy-done.15, f32[8,64,1891]{2,1,0:T(8,128)S(1)} %get-tuple-element.438, f32[8,64,1891]{2,1,0:T(8,128)S(1)} %get-tuple-element.439, f32[62,3782]{1,0:T(8,128)S(1)} %copy-done.13, ...), kind=kOutput, calls=%fused_computation.22.clone.1 | convolution fusion | flops 1442764800 | bytes 9895940 | tf_op jit(solution)/shard_map/while/body/eval_jaxpr/kdb,sb->kds/dot_general | solution.py:138
  97.3 3.3 fusion.137
  101.0 3.3 fusion.138
  113.5 2.4 reduce_sum.33
  117.0 3.4 add_dynamic-update-slice_fusion.102
  133.2 9.5 %fusion.140 = f32[8,64,62]{2,1,0:T(8,128)S(1)} fusion(f32[8,64,1891]{2,1,0:T(8,128)} %broadcast_multiply_fusion.7, f32[8,64,1891]{2,1,0:T(8,128)} %broadcast_multiply_fusion.8, f32[62,3782]{1,0:T(8,128)S(1)} %copy-done.12, f32[1,8,64,62]{3,2,1,0:T(8,128)S(1)} %copy.36, f32[1,8,64,62]{3,2,1,0:T(8,128)S(1)} %copy-done.17, ...), kind=kOutput, calls=%fused_computation.24.clone.1 | convolution fusion | flops 1442764800 | bytes 9191380 | tf_op jit(solution)/shard_map/while/body/eval_jaxpr/kdb,sb->kds/dot_general | solution.py:138
  142.7 3.3 fusion.141
  146.1 3.3 fusion.142
  162.1 3.4 add_dynamic-update-slice_fusion.125
  172.2 6.3 %fusion.143 = f32[2,8,64,62]{3,2,1,0:T(8,128)S(1)} fusion(f32[2,8,64,62]{3,2,1,0:T(8,128)S(1)} %copy-done.24, s32[]{:T(128)S(6)} %copy.82, f32[8,64,62]{2,1,0:T(8,128)S(1)} %copy-done.15, f32[8,64,1891]{2,1,0:T(8,128)S(1)} %get-tuple-element.438, f32[8,64,1891]{2,1,0:T(8,128)S(1)} %get-tuple-element.439, f32[62,3782]{1,0:T(8,128)S(1)} %copy-done.13, ...), kind=kOutput, calls=%fused_computation.22.clone.1 | convolution fusion | flops 1442764800 | bytes 9895940 | tf_op jit(solution)/shard_map/while/body/eval_jaxpr/kdb,sb->kds/dot_general | solution.py:138
  186.7 3.9 %fusion.80 = f32[3,8,64,62]{2,0,3,1:T(4,128)} fusion(f32[2,8,64,62]{2,0,3,1:T(2,128)S(1)} %copy.25, f32[1,2]{0,1:T(2,128)} %copy-done.30, f32[1,2]{0,1:T(2,128)} %copy-done.28, f32[1,2]{0,1:T(2,128)} %copy-done.32), kind=kOutput, calls=%fused_computation.190 | convolution fusion | flops 2285580 | bytes 634904 | tf_op jit(solution)/shard_map/ic,ckds->ikds/dot_general | solution.py:150
  200.2 98.4 %all-reduce.3.cloned.1.call-done = f32[3,8,64,62]{2,0,3,1:T(4,128)} async-done(((f32[3,8,64,62]{2,0,3,1:T(4,128)}), f32[3,8,64,62]{2,0,3,1:T(4,128)}) %all-reduce.3.cloned.1.call-update) | async-done | bytes 380944 | tf_op jit(solution)/shard_map/psum | solution.py:153
  315.5 29.8 %all-reduce.5.cloned.1.call-done = f32[3,8,64,62]{2,0,3,1:T(4,128)} async-done(((f32[3,8,64,62]{2,0,3,1:T(4,128)}), f32[3,8,64,62]{2,0,3,1:T(4,128)}) %all-reduce.5.cloned.1.call-update) | async-done | bytes 380944 | tf_op jit(solution)/shard_map/psum | solution.py:154
  345.3 3.7 %fusion.77 = f32[3,8,64,62]{2,0,3,1:T(4,128)S(1)} fusion(f32[3,8,64,62]{2,0,3,1:T(4,128)} %all-reduce.5.cloned.1.call-done, f32[1,3]{0,1:T(4,128)S(1)} %copy.14, f32[1,3]{0,1:T(4,128)S(1)} %copy.13, f32[1,3]{0,1:T(4,128)S(1)} %copy.12, f32[]{:T(128)} %get-tuple-element.201), kind=kOutput, calls=%fused_computation.186 | convolution fusion | flops 3428379 | bytes 761896 | tf_op jit(solution)/shard_map/ij,jkds->ikds/dot_general | solution.py:155
  (268 shorter events, 100.4 us)
Async XLA Ops:
  7.2 291.4 %all-reduce.3.cloned.1.call-start = ((), (), s32[]{:S(2)}) async-start(), calls=%async_computation | async-start | bytes 2031616 | tf_op jit(solution)/shard_map/psum | solution.py:153
  7.2 5.0 %copy-start.28 = (f32[1,2]{0,1:T(2,128)}, f32[1,2]{0,1:T(2,128)S(1)}, u32[]{:S(2)}) copy-start(f32[1,2]{0,1:T(2,128)S(1)} %get-tuple-element.225) | copy-start | bytes 28
  7.2 4.9 %copy-start.30 = (f32[1,2]{0,1:T(2,128)}, f32[1,2]{0,1:T(2,128)S(1)}, u32[]{:S(2)}) copy-start(f32[1,2]{0,1:T(2,128)S(1)} %get-tuple-element.226) | copy-start | bytes 28
  7.3 4.9 %copy-start.32 = (f32[1,2]{0,1:T(2,128)}, f32[1,2]{0,1:T(2,128)S(1)}, u32[]{:S(2)}) copy-start(f32[1,2]{0,1:T(2,128)S(1)} %fusion.87) | copy-start | bytes 28
  16.9 11.8 %copy-start.2 = (f32[8,64,1891]{2,1,0:T(8,128)}, f32[8,64,1891]{2,1,0:T(8,128)S(1)}, u32[]{:S(2)}) copy-start(f32[8,64,1891]{2,1,0:T(8,128)S(1)} %fusion.137) | copy-start | bytes 11618308 | tf_op jit(solution)/shard_map/while
  17.3 8.0 %copy-start.4 = (f32[1,8,64,1891]{3,2,1,0:T(8,128)}, f32[1,8,64,1891]{3,2,1,0:T(8,128)S(1)}, u32[]{:S(2)}) copy-start(f32[1,8,64,1891]{3,2,1,0:T(8,128)S(1)} %dynamic-slice_convert_fusion.2) | copy-start | bytes 11618308 | tf_op jit(solution)/shard_map/while
  33.3 5.1 %copy-start.5 = (f32[1,8,64,1891]{3,2,1,0:T(8,128)S(1)}, f32[1,8,64,1891]{3,2,1,0:T(8,128)}, u32[]{:S(2)}) copy-start(f32[1,8,64,1891]{3,2,1,0:T(8,128)} %copy-done.4) | copy-start | bytes 11618308 | tf_op jit(solution)/shard_map/while
  49.8 9.5 %copy-start.18 = (f32[1,8,64,62]{3,2,1,0:T(8,128)}, f32[1,8,64,62]{3,2,1,0:T(8,128)S(1)}, u32[]{:S(2)}) copy-start(f32[1,8,64,62]{3,2,1,0:T(8,128)S(1)} %copy.36) | copy-start | bytes 380932 | tf_op jit(solution)/shard_map/while
  59.3 6.7 %copy-start.6 = (f32[1,8,64,1891]{3,2,1,0:T(8,128)S(1)}, f32[1,8,64,1891]{3,2,1,0:T(8,128)}, u32[]{:S(2)}) copy-start(f32[1,8,64,1891]{3,2,1,0:T(8,128)} %copy-done.4) | copy-start | bytes 11618308 | tf_op jit(solution)/shard_map/while
  62.7 11.4 %copy-start = (f32[8,64,1891]{2,1,0:T(8,128)}, f32[8,64,1891]{2,1,0:T(8,128)S(1)}, u32[]{:S(2)}) copy-start(f32[8,64,1891]{2,1,0:T(8,128)S(1)} %fusion.141) | copy-start | bytes 11618308 | tf_op jit(solution)/shard_map/while
  78.6 5.1 %copy-start.7 = (f32[1,8,64,1891]{3,2,1,0:T(8,128)S(1)}, f32[1,8,64,1891]{3,2,1,0:T(8,128)}, u32[]{:S(2)}) copy-start(f32[1,8,64,1891]{3,2,1,0:T(8,128)} %copy-done.4) | copy-start | bytes 11618308 | tf_op jit(solution)/shard_map/while
  100.7 11.8 %copy-start.2 = (f32[8,64,1891]{2,1,0:T(8,128)}, f32[8,64,1891]{2,1,0:T(8,128)S(1)}, u32[]{:S(2)}) copy-start(f32[8,64,1891]{2,1,0:T(8,128)S(1)} %fusion.137) | copy-start | bytes 11618308 | tf_op jit(solution)/shard_map/while
  101.0 8.0 %copy-start.4 = (f32[1,8,64,1891]{3,2,1,0:T(8,128)}, f32[1,8,64,1891]{3,2,1,0:T(8,128)S(1)}, u32[]{:S(2)}) copy-start(f32[1,8,64,1891]{3,2,1,0:T(8,128)S(1)} %dynamic-slice_convert_fusion.2) | copy-start | bytes 11618308 | tf_op jit(solution)/shard_map/while
  117.0 5.1 %copy-start.5 = (f32[1,8,64,1891]{3,2,1,0:T(8,128)S(1)}, f32[1,8,64,1891]{3,2,1,0:T(8,128)}, u32[]{:S(2)}) copy-start(f32[1,8,64,1891]{3,2,1,0:T(8,128)} %copy-done.4) | copy-start | bytes 11618308 | tf_op jit(solution)/shard_map/while
  133.2 9.5 %copy-start.18 = (f32[1,8,64,62]{3,2,1,0:T(8,128)}, f32[1,8,64,62]{3,2,1,0:T(8,128)S(1)}, u32[]{:S(2)}) copy-start(f32[1,8,64,62]{3,2,1,0:T(8,128)S(1)} %copy.36) | copy-start | bytes 380932 | tf_op jit(solution)/shard_map/while
  142.7 6.7 %copy-start.6 = (f32[1,8,64,1891]{3,2,1,0:T(8,128)S(1)}, f32[1,8,64,1891]{3,2,1,0:T(8,128)}, u32[]{:S(2)}) copy-start(f32[1,8,64,1891]{3,2,1,0:T(8,128)} %copy-done.4) | copy-start | bytes 11618308 | tf_op jit(solution)/shard_map/while
  146.1 11.4 %copy-start = (f32[8,64,1891]{2,1,0:T(8,128)}, f32[8,64,1891]{2,1,0:T(8,128)S(1)}, u32[]{:S(2)}) copy-start(f32[8,64,1891]{2,1,0:T(8,128)S(1)} %fusion.141) | copy-start | bytes 11618308 | tf_op jit(solution)/shard_map/while
  162.1 5.1 %copy-start.7 = (f32[1,8,64,1891]{3,2,1,0:T(8,128)S(1)}, f32[1,8,64,1891]{3,2,1,0:T(8,128)}, u32[]{:S(2)}) copy-start(f32[1,8,64,1891]{3,2,1,0:T(8,128)} %copy-done.4) | copy-start | bytes 11618308 | tf_op jit(solution)/shard_map/while
  185.1 113.5 %copy-start.26 = (f32[2,8,64,62]{3,2,1,0:T(8,128)S(1)}, f32[2,8,64,62]{3,2,1,0:T(8,128)}, u32[]{:S(2)}) copy-start(f32[2,8,64,62]{3,2,1,0:T(8,128)} %get-tuple-element.108) | copy-start | bytes 761860
  190.6 159.4 %copy-start.27 = (f32[2,8,64,62]{2,1,3,0:T(8,128)S(1)}, f32[2,8,64,62]{2,1,3,0:T(8,128)}, u32[]{:S(2)}) copy-start(f32[2,8,64,62]{2,1,3,0:T(8,128)} %param.12) | copy-start | bytes 761860
  190.6 159.4 %copy-start.29 = (f32[1,2]{0,1:T(2,128)S(1)}, f32[1,2]{0,1:T(2,128)}, u32[]{:S(2)}) copy-start(f32[1,2]{0,1:T(2,128)} %copy-done.28) | copy-start | bytes 28
  190.6 159.4 %copy-start.31 = (f32[1,2]{0,1:T(2,128)S(1)}, f32[1,2]{0,1:T(2,128)}, u32[]{:S(2)}) copy-start(f32[1,2]{0,1:T(2,128)} %copy-done.30) | copy-start | bytes 28
  190.6 159.4 %copy-start.33 = (f32[1,2]{0,1:T(2,128)S(1)}, f32[1,2]{0,1:T(2,128)}, u32[]{:S(2)}) copy-start(f32[1,2]{0,1:T(2,128)} %copy-done.32) | copy-start | bytes 28
  190.6 154.7 %all-reduce.5.cloned.1.call-start = ((), (), s32[]{:S(2)}) async-start(), calls=%async_computation.1 | async-start | bytes 2031616 | tf_op jit(solution)/shard_map/psum | solution.py:154
  (38 other events, 95.5 us)
Sparse Core Ops, SparseCore 0:
  190.8 107.7 all-reduce.2
  301.1 44.1 all-reduce.4
where the time goes:
time: 363 us; the launch traced here: 360 us
  waiting for transfers between devices  128 us (35%)
  other arithmetic  90.9 us (25%)
  matrix products  71.9 us (20%)
  between operations  36.4 us (10%)
  local copies, waits for them, and re-layouts  24.2 us (7%)
  loops' own time  8.49 us (2%)
    psum x1, waiting for transfers between devices, shards(): group_sums = lax.psum(local_sums, 'chan')  98.4 us
    while x80, other arithmetic  55 us
    dot_general x4, matrix products, spread(): jnp.einsum('kdb,sb->kds', joined, both_tables, precision=HIGHEST_PRECISION)  31.6 us
    psum x1, waiting for transfers between devices, shards(): sums = lax.psum(group_sums, 'grp')  29.8 us
    dot_general x4, matrix products, collect(): jnp.einsum('kds,sb->kdb', jones, first_table, precision=HIGHEST_PRECISION)  13.3 us
    dot_general x4, matrix products, collect(): jnp.einsum('kds,sb->kdb', jones, second_table, precision=HIGHEST_PRECISION)  13.3 us
    while x104, local copies, waits for them, and re-layouts  11.9 us
    reduce_sum x4, other arithmetic, data_gradient(): jnp.sum(as_stacked(matrix_product(propagated, adjoint(second_terms))), ax...  9.71 us
  transfers between devices with their start and end apart: 2, of which 2 were waited for; matrix products, arithmetic and copies ran while one was open for 1% of the time, Pallas kernels for 0%

commit v1 on v0

v1 whole, which is shorter than its diff:
```python
import functools

import jax
import jax.numpy as jnp
import numpy as np
from jax import lax
from jax.experimental import pallas as pl
from jax.experimental.pallas import tpu as pltpu
from jax.sharding import PartitionSpec as P

SAMPLES = 16
STEPS = 2
ETA_STEP = 0.08
RHO_PENALTY = 1.0
GROUP = 128
TILE = 384
HALF = 32
F32 = jnp.float32
BF16 = jnp.bfloat16
HIGHEST_PRECISION = lax.Precision.HIGHEST


def bernstein(position):
    return [
        (1.0 - position) * (1.0 - position),
        2.0 * position * (1.0 - position),
        position * position,
    ]


def gram_inverse(channels):
    position = (np.arange(channels, dtype=np.float64) + 0.5) / channels
    values = np.stack(bernstein(position))
    matrix = values @ values.T
    rows = [np.cross(matrix[1], matrix[2]), np.cross(matrix[2], matrix[0]), np.cross(matrix[0], matrix[1])]
    return np.stack(rows).T / np.sum(matrix[0] * rows[0])


def product(a, b):
    out = []
    for row in range(2):
        for col in range(2):
            lr, li = a[4 * row], a[4 * row + 1]
            mr, mi = a[4 * row + 2], a[4 * row + 3]
            br, bi = b[2 * col], b[2 * col + 1]
            dr, di = b[4 + 2 * col], b[4 + 2 * col + 1]
            out.append((lr * br - li * bi) + (mr * dr - mi * di))
            out.append((lr * bi + li * br) + (mr * di + mi * dr))
    return out


def product_adjoint(a, b):
    out = []
    for row in range(2):
        for col in range(2):
            lr, li = a[4 * row], a[4 * row + 1]
            mr, mi = a[4 * row + 2], a[4 * row + 3]
            br, bi = b[4 * col], b[4 * col + 1]
            dr, di = b[4 * col + 2], b[4 * col + 3]
            out.append((lr * br + li * bi) + (mr * dr + mi * di))
            out.append((li * br - lr * bi) + (mi * dr - mr * di))
    return out


def adjoint_product(a, b):
    out = []
    for row in range(2):
        for col in range(2):
            lr, li = a[2 * row], a[2 * row + 1]
            mr, mi = a[4 + 2 * row], a[4 + 2 * row + 1]
            br, bi = b[2 * col], b[2 * col + 1]
            dr, di = b[4 + 2 * col], b[4 + 2 * col + 1]
            out.append((lr * br + li * bi) + (mr * dr + mi * di))
            out.append((lr * bi - li * br) + (mr * di - mi * dr))
    return out


def split(value):
    high = value.astype(BF16)
    low = (value - high.astype(F32)).astype(BF16)
    return high, low


def descend_kernel(
    channels, blocks, pairs_ref, counts_ref, jones_ref, duals_ref, consensus_ref, vis_ref, coh_ref,
    jones_out, sums_out,
    pairs_pad, vis_pad, coh_tail, gather_hot, spread_hot, jones_cur, jones_split, base, first_all,
    second_all, propagated_all, partial_pred, residual_all, grad_parts,
):
    own, _, dirs, stations = jones_ref.shape
    count = pairs_ref.shape[1]
    tiles = gather_hot.shape[0]
    full = (count // GROUP) * GROUP
    halves = dirs // HALF
    chunks = own * halves
    per_tile = TILE // GROUP
    offset = (lax.axis_index("grp") * blocks + lax.axis_index("chan")) * own

    pairs_pad[...] = jnp.full(pairs_pad.shape, -1, jnp.int32)
    pairs_pad[0:2, 0:count] = pairs_ref[...]
    vis_pad[...] = jnp.zeros(vis_pad.shape, F32)
    vis_pad[:, :, 0:count] = vis_ref[...]
    coh_tail[...] = jnp.zeros(coh_tail.shape, BF16)
    coh_tail[:, :, :, 0 : count - full] = coh_ref[:, :, :, full:count]

    ids = lax.broadcasted_iota(jnp.int32, (GROUP, GROUP), 0)
    for tile in range(tiles):
        for part in range(per_tile):
            lanes = slice(tile * TILE + part * GROUP, tile * TILE + (part + 1) * GROUP)
            for side in range(2):
                row = pairs_pad[side : side + 1, lanes]
                hot = jnp.where(ids == row, 1.0, 0.0).astype(BF16)
                where = side * TILE + part * GROUP
                gather_hot[tile, 0:GROUP, where : where + GROUP] = hot
                gather_hot[tile, GROUP : 2 * GROUP, where : where + GROUP] = hot
                for half in range(2):
                    where = (2 * side + half) * TILE + part * GROUP
                    spread_hot[tile, :, where : where + GROUP] = hot

    jones_cur[...] = jnp.zeros(jones_cur.shape, F32)
    base[...] = jnp.zeros(base.shape, F32)
    basis = []
    for channel in range(own):
        position = ((offset + channel).astype(F32) + 0.5) * (1.0 / channels)
        basis.append(bernstein(position))
        for half in range(halves):
            where = slice(half * HALF, (half + 1) * HALF)
            chunk = channel * halves + half
            target = sum(basis[channel][i] * consensus_ref[i, :, where, :] for i in range(3))
            base[chunk, :, :, 0:stations] = ETA_STEP * (RHO_PENALTY * target - duals_ref[channel, :, where, :])
            jones_cur[chunk, :, :, 0:stations] = jones_ref[channel, :, where, :]

    def divide(chunk):
        value = jones_cur[chunk].reshape(8 * HALF, GROUP)
        high, low = split(value)
        jones_split[chunk, :, 0:GROUP] = high
        jones_split[chunk, :, GROUP : 2 * GROUP] = low

    for chunk in range(chunks):
        divide(chunk)

    def coherency(channel, comp, start, group):
        if group * GROUP < full:
            value = coh_ref[channel, comp, pl.ds(start, 16), group * GROUP : (group + 1) * GROUP]
        else:
            value = coh_tail[channel, comp, pl.ds(start, 16), :]
        return value.astype(F32)

    def predict(chunk, _):
        channel, half = chunk // halves, chunk % halves
        for tile in range(tiles):
            both = jnp.dot(jones_split[chunk], gather_hot[tile], preferred_element_type=F32)
            first_all[tile] = both[:, 0:TILE]
            second_all[chunk, tile] = both[:, TILE : 2 * TILE]
            for part in range(per_tile):
                group = tile * per_tile + part
                lanes = slice(part * GROUP, (part + 1) * GROUP)
                total = None
                for deep in range(HALF // 16):
                    start = pl.multiple_of(half * HALF + deep * 16, 16)
                    rows = [slice(c * HALF + deep * 16, c * HALF + deep * 16 + 16) for c in range(8)]
                    source = [coherency(channel, c, start, group) for c in range(8)]
                    first = [first_all[tile, rows[c], lanes] for c in range(8)]
                    second = [second_all[chunk, tile, rows[c], lanes] for c in range(8)]
                    propagated = product(first, source)
                    for c in range(8):
                        propagated_all[chunk, tile, rows[c], lanes] = propagated[c]
                    model = product_adjoint(propagated, second)
                    model = [m[0:8] + m[8:16] for m in model]
                    total = model if total is None else [t + m for t, m in zip(total, model)]
                for c in range(8):
                    partial_pred[chunk, c, :, group * GROUP : (group + 1) * GROUP] = total[c]
        return 0

    def correct(chunk, _):
        channel, half = chunk // halves, chunk % halves
        total = None
        for tile in range(tiles):
            for part in range(per_tile):
                group = tile * per_tile + part
                lanes = slice(part * GROUP, (part + 1) * GROUP)
                residual = [
                    jnp.broadcast_to(
                        residual_all[channel, c : c + 1, group * GROUP : (group + 1) * GROUP], (16, GROUP)
                    )
                    for c in range(8)
                ]
                for deep in range(HALF // 16):
                    start = pl.multiple_of(half * HALF + deep * 16, 16)
                    rows = [slice(c * HALF + deep * 16, c * HALF + deep * 16 + 16) for c in range(8)]
                    source = [coherency(channel, c, start, group) for c in range(8)]
                    second = [second_all[chunk, tile, rows[c], lanes] for c in range(8)]
                    conjugated = product_adjoint(second, source)
                    grad_first = product(residual, conjugated)
                    for c in range(8):
                        high, low = split(grad_first[c])
                        grad_parts[tile, rows[c], part * GROUP : (part + 1) * GROUP] = high
                        grad_parts[tile, rows[c], TILE + part * GROUP : TILE + (part + 1) * GROUP] = low
                    propagated = [propagated_all[chunk, tile, rows[c], lanes] for c in range(8)]
                    grad_second = adjoint_product(residual, propagated)
                    for c in range(8):
                        high, low = split(grad_second[c])
                        grad_parts[tile, rows[c], 2 * TILE + part * GROUP : 2 * TILE + (part + 1) * GROUP] = high
                        grad_parts[tile, rows[c], 3 * TILE + part * GROUP : 3 * TILE + (part + 1) * GROUP] = low
            piece = lax.dot_general(
                grad_parts[tile], spread_hot[tile], (((1,), (1,)), ((), ())), preferred_element_type=F32
            )
            total = piece if total is None else total + piece
        update = total.reshape(8, HALF, GROUP)
        jones_cur[chunk] = (1.0 - ETA_STEP * RHO_PENALTY) * jones_cur[chunk] + base[chunk] + update
        divide(chunk)
        return 0

    for _ in range(STEPS):
        lax.fori_loop(0, chunks, predict, 0)
        for channel in range(own):
            factor = counts_ref[channel].astype(F32) * (2.0 * ETA_STEP / SAMPLES)
            for group in range(tiles * per_tile):
                lanes = slice(group * GROUP, (group + 1) * GROUP)
                total = sum(partial_pred[channel * halves + half, :, :, lanes] for half in range(halves))
                residual_all[channel, :, lanes] = (vis_pad[channel, :, lanes] - jnp.sum(total, axis=1)) * factor
        lax.fori_loop(0, chunks, correct, 0)

    for half in range(halves):
        where = slice(half * HALF, (half + 1) * HALF)
        jones = [jones_cur[channel * halves + half][:, :, 0:stations] for channel in range(own)]
        joined = [jones[channel] + duals_ref[channel, :, where, :] * (1.0 / RHO_PENALTY) for channel in range(own)]
        for channel in range(own):
            jones_out[channel, :, where, :] = jones[channel]
        for i in range(3):
            sums_out[i, :, where, :] = sum(basis[channel][i] * joined[channel] for channel in range(own))


def descend(channels, blocks, pairs, counts, jones, duals, consensus, visibilities, coherencies):
    own, _, dirs, stations = jones.shape
    count = pairs.shape[1]
    tiles = -(-count // TILE)
    lanes = tiles * TILE
    chunks = own * (dirs // HALF)
    rows = 8 * HALF
    vmem = pl.BlockSpec(memory_space=pltpu.VMEM)
    smem = pl.BlockSpec(memory_space=pltpu.SMEM)
    return pl.pallas_call(
        functools.partial(descend_kernel, channels, blocks),
        out_shape=(
            jax.ShapeDtypeStruct(jones.shape, F32),
            jax.ShapeDtypeStruct(consensus.shape, F32),
        ),
        in_specs=[vmem, smem, vmem, vmem, vmem, vmem, vmem],
        out_specs=(vmem, vmem),
        scratch_shapes=[
            pltpu.VMEM((8, lanes), jnp.int32),
            pltpu.VMEM((own, 8, lanes), F32),
            pltpu.VMEM((own, 8, dirs, GROUP), BF16),
            pltpu.VMEM((tiles, 2 * GROUP, 2 * TILE), BF16),
            pltpu.VMEM((tiles, GROUP, 4 * TILE), BF16),
            pltpu.VMEM((chunks, 8, HALF, GROUP), F32),
            pltpu.VMEM((chunks, rows, 2 * GROUP), BF16),
            pltpu.VMEM((chunks, 8, HALF, GROUP), F32),
            pltpu.VMEM((tiles, rows, TILE), F32),
            pltpu.VMEM((chunks, tiles, rows, TILE), F32),
            pltpu.VMEM((chunks, tiles, rows, TILE), F32),
            pltpu.VMEM((chunks, 8, 8, lanes), F32),
            pltpu.VMEM((own, 8, lanes), F32),
            pltpu.VMEM((tiles, rows, 4 * TILE), BF16),
        ],
        compiler_params=pltpu.CompilerParams(vmem_limit_bytes=56 * 2**20),
        name="descend",
    )(pairs, counts, jones, duals, consensus, visibilities, coherencies)


def shards(jones_start, duals_start, consensus_start, visibilities, coherencies, pairs, counts):
    own = jones_start.shape[0]
    blocks = lax.axis_size("chan")
    channels = own * lax.axis_size("grp") * blocks
    offset = (lax.axis_index("grp") * blocks + lax.axis_index("chan")) * own
    jones, local_sums = descend(
        channels, blocks, pairs, counts, jones_start, duals_start, consensus_start, visibilities, coherencies
    )
    sums = lax.psum(local_sums, ("grp", "chan"))
    inverse = gram_inverse(channels).astype(np.float32)
    consensus = jnp.stack([sum(inverse[i, j] * sums[j] for j in range(3)) for i in range(3)])
    duals = []
    for channel in range(own):
        position = ((offset + channel).astype(F32) + 0.5) * (1.0 / channels)
        basis = bernstein(position)
        smooth = sum(basis[i] * consensus[i] for i in range(3))
        duals.append(duals_start[channel] + RHO_PENALTY * (jones[channel] - smooth))
    return (jones, jnp.stack(duals), consensus)


def solution(mesh):
    in_specs = (
        P(("grp", "chan"), None, None, None),
        P(("grp", "chan"), None, None, None),
        P(),
        P(("grp", "chan"), None, None),
        P(("grp", "chan"), None, None, None),
        P(),
        P(("grp", "chan")),
    )
    out_specs = (P(("grp", "chan"), None, None, None), P(("grp", "chan"), None, None, None), P())
    return jax.shard_map(shards, mesh=mesh, in_specs=in_specs, out_specs=out_specs, check_vma=False)
```

time: 363 us -> 221 us (0.61)
  other arithmetic: 90.9 us -> 1.6 us
  matrix products: 71.9 us -> 0 us
  Pallas kernels: 0 us -> 46.7 us
  between operations: 36.4 us -> 14.1 us
  waiting for transfers between devices: 128 us -> 148 us
  local copies, waits for them, and re-layouts: 24.2 us -> 10.8 us
  loops' own time: 8.49 us -> 0 us
    dot_general x18 -> x0, matrix products: 71.9 us -> none  [the longest x4 31.6 us: spread(): jnp.einsum('kdb,sb->kds', joined, both_tables, precision=HIGHEST_PRECISION)]
    while x80 -> x0, other arithmetic: 55 us -> none
    pallas_call x0 -> x1, Pallas kernels: none -> 46.7 us  [descend(): pl.pallas_call(functools.partial(descend_kernel, channels, blocks), out_s...]
    psum x2 -> x1, waiting for transfers between devices: 128 us -> 148 us  [shards(): sums = lax.psum(local_sums, ('grp', 'chan'))]
    while x105 -> x0, local copies, waits for them, and re-layouts: 12.2 us -> none
    mul x10 -> x0, other arithmetic: 10.5 us -> none  [the longest x4 5.87 us: data_gradient(): factor * as_stacked(matrix_product(adjoint(residual), propagated))]
    reduce_sum x5 -> x0, other arithmetic: 10.4 us -> none  [the longest x4 9.71 us: data_gradient(): jnp.sum(as_stacked(matrix_product(propagated, adjoint(second_terms))), ax...]
    another operation x1 -> x0, loops' own time: 8.49 us -> none  [shards(): lax.map(update, (jones, duals, coherencies, visibilities, weights, basis_...]
  transfers between devices with their start and end apart: 2 -> 1, of which waited for: 2 -> 1; matrix products, arithmetic and copies ran while one was open for 1% -> 1% of each run, Pallas kernels for 0% -> 0%
where the time goes in v1:
time: 221 us
  waiting for transfers between devices  148 us (67%)
  Pallas kernels  46.7 us (21%)
  between operations  14.1 us (6%)
  local copies, waits for them, and re-layouts  10.8 us (5%)
    psum x1, waiting for transfers between devices, shards(): sums = lax.psum(local_sums, ('grp', 'chan'))  148 us
    pallas_call x1, Pallas kernels, descend(): pl.pallas_call(functools.partial(descend_kernel, channels, blocks), out_s...  46.7 us
    unnamed x10, local copies, waits for them, and re-layouts  10.8 us
  transfers between devices with their start and end apart: 1, of which 1 were waited for; matrix products, arithmetic and copies ran while one was open for 1% of the time, Pallas kernels for 0%

profile of v1, /device:TPU:1, one launch (start us, length us, event | category | flops | bytes accessed | tf_op | source)
XLA Modules:
  0.0 220.8 jit_solution(15565575257563690751)
XLA Ops:
  7.2 0.0 all-reduce.2.cloned.1.call-start
  7.2 2.0 copy.11.duals_ref
  9.3 2.1 copy.10.jones_ref
  11.3 2.3 %copy.12.consensus_ref = f32[3,8,64,62]{3,2,1,0:T(8,128)} copy(f32[3,8,64,62]{2,1,3,0:T(8,128)} %param.9) | data formatting | bytes 761856 | tf_op args[2]
  13.6 0.0 copy-start
  13.6 46.7 %descend.1 = (f32[2,8,64,62]{3,2,1,0:T(8,128)}, f32[3,8,64,62]{3,2,1,0:T(8,128)}) custom-call(s32[2,1891]{1,0:T(2,128)} %pairs_ref.1, s32[2]{0:T(128)} %counts_ref.1, f32[2,8,64,62]{3,2,1,0:T(8,128)} %copy.10.jones_ref, f32[2,8,64,62]{3,2,1,0:T(8,128)} %copy.11.duals_ref, f32[3,8,64,62]{3,2,1,0:T(8,128)} %copy.12.consensus_ref, f32[2,8,1891]{2,1,0:T(8,128)} %vis_ref.1, ...), custom_call_target="tpu_custom_call" | custom-call | tf_op jit(solution)/shard_map/descend/pallas_call | solution.py:243
  60.3 0.0 copy-start.1
  60.3 0.0 all-reduce.2.cloned.1.call-update
  60.4 2.1 copy.15
  62.5 147.7 %all-reduce.2.cloned.1.call-done = f32[3,8,64,62]{3,2,1,0:T(8,128)} async-done(((f32[3,8,64,62]{3,2,1,0:T(8,128)}), f32[3,8,64,62]{3,2,1,0:T(8,128)}) %all-reduce.2.cloned.1.call-update) | async-done | bytes 380944 | tf_op jit(solution)/shard_map/psum | solution.py:280
  210.1 0.0 copy-done
  210.2 1.4 slice_add_fusion.1
  211.6 0.1 pad_maximum_fusion
  211.6 0.0 copy-done.1
  211.6 0.1 slice_add_fusion
  211.8 1.0 copy.16
  212.8 1.2 copy.17
  (1 shorter events, 0.0 us)
Async XLA Ops:
  7.2 203.0 %all-reduce.2.cloned.1.call-start = ((), (), s32[]{:S(2)}) async-start(), calls=%async_computation | async-start | bytes 1572864 | tf_op jit(solution)/shard_map/psum | solution.py:280
  13.6 196.5 %copy-start = (f32[2,8,64,62]{3,2,1,0:T(8,128)S(1)}, f32[2,8,64,62]{3,2,1,0:T(8,128)}, u32[]{:S(2)}) copy-start(f32[2,8,64,62]{3,2,1,0:T(8,128)} %copy.11.duals_ref) | copy-start | bytes 761860
  60.3 151.3 %copy-start.1 = (f32[2,8,64,62]{3,2,1,0:T(8,128)S(1)}, f32[2,8,64,62]{3,2,1,0:T(8,128)}, u32[]{:S(2)}) copy-start(f32[2,8,64,62]{3,2,1,0:T(8,128)} %get-tuple-element.7) | copy-start | bytes 761860
Sparse Core Ops, SparseCore 0:
  60.5 149.6 all-reduce.1

commit v2 on v1

v2 whole, which is shorter than its diff:
```python
import functools

import jax
import jax.numpy as jnp
import numpy as np
from jax import lax
from jax.experimental import pallas as pl
from jax.experimental.pallas import tpu as pltpu
from jax.sharding import PartitionSpec as P

SAMPLES = 16
STEPS = 2
ETA_STEP = 0.08
RHO_PENALTY = 1.0
GROUP = 128
F32 = jnp.float32
BF16 = jnp.bfloat16
MESH = pl.DeviceIdType.MESH
SIDE = 4


def bernstein(position):
    return [
        (1.0 - position) * (1.0 - position),
        2.0 * position * (1.0 - position),
        position * position,
    ]


def gram_inverse(channels):
    position = (np.arange(channels, dtype=np.float64) + 0.5) / channels
    values = np.stack(bernstein(position))
    matrix = values @ values.T
    rows = [np.cross(matrix[1], matrix[2]), np.cross(matrix[2], matrix[0]), np.cross(matrix[0], matrix[1])]
    return np.stack(rows).T / np.sum(matrix[0] * rows[0])


def product_terms(a, b):
    for row in range(2):
        for col in range(2):
            lr, li = a[4 * row], a[4 * row + 1]
            mr, mi = a[4 * row + 2], a[4 * row + 3]
            br, bi = b[2 * col], b[2 * col + 1]
            dr, di = b[4 + 2 * col], b[4 + 2 * col + 1]
            yield ((lr * br - li * bi) + (mr * dr - mi * di))
            yield ((lr * bi + li * br) + (mr * di + mi * dr))


def product(a, b):
    return list(product_terms(a, b))


def product_adjoint_terms(a, b):
    for row in range(2):
        for col in range(2):
            lr, li = a[4 * row], a[4 * row + 1]
            mr, mi = a[4 * row + 2], a[4 * row + 3]
            br, bi = b[4 * col], b[4 * col + 1]
            dr, di = b[4 * col + 2], b[4 * col + 3]
            yield ((lr * br + li * bi) + (mr * dr + mi * di))
            yield ((li * br - lr * bi) + (mi * dr - mr * di))


def product_adjoint(a, b):
    return list(product_adjoint_terms(a, b))


def adjoint_product_terms(a, b):
    for row in range(2):
        for col in range(2):
            lr, li = a[2 * row], a[2 * row + 1]
            mr, mi = a[4 + 2 * row], a[4 + 2 * row + 1]
            br, bi = b[2 * col], b[2 * col + 1]
            dr, di = b[4 + 2 * col], b[4 + 2 * col + 1]
            yield ((lr * br + li * bi) + (mr * dr + mi * di))
            yield ((lr * bi - li * br) + (mr * di - mi * dr))


def adjoint_product(a, b):
    return list(adjoint_product_terms(a, b))


def split(value):
    high = value.astype(BF16)
    low = (value - high.astype(F32)).astype(BF16)
    return high, low


def descend_kernel(
    channels, blocks, pairs_ref, counts_ref, jones_ref, duals_ref, consensus_ref, vis_ref, coh_ref,
    jones_out, sums_out,
    pairs_pad, vis_pad, coh_tail, gather_hot, spread_hot, jones_cur, jones_split, base, turned, both_now,
    propagated_now, grad_parts, update_now,
):
    own, stations, _, dirs = jones_ref.shape
    count = pairs_ref.shape[1]
    groups = gather_hot.shape[0]
    full = count // GROUP
    rows = 8 * dirs
    offset = (lax.axis_index("grp") * blocks + lax.axis_index("chan")) * own

    pairs_pad[...] = jnp.full(pairs_pad.shape, -1, jnp.int32)
    pairs_pad[0:2, 0:count] = pairs_ref[...]
    vis_pad[...] = jnp.zeros(vis_pad.shape, F32)
    vis_pad[:, :, 0:count] = vis_ref[...]
    coh_tail[...] = jnp.zeros(coh_tail.shape, BF16)
    coh_tail[:, :, :, 0 : count - full * GROUP] = coh_ref[:, :, :, full * GROUP : count]

    ids = lax.broadcasted_iota(jnp.int32, (GROUP, GROUP), 0)
    for group in range(groups):
        for side in range(2):
            row = pairs_pad[side : side + 1, group * GROUP : (group + 1) * GROUP]
            hot = jnp.where(ids == row, 1.0, 0.0).astype(BF16)
            for part in range(2):
                gather_hot[group, part * GROUP : (part + 1) * GROUP, side * GROUP : (side + 1) * GROUP] = hot
                where = (2 * side + part) * GROUP
                spread_hot[group, :, where : where + GROUP] = hot

    basis = []
    for channel in range(own):
        position = ((offset + channel).astype(F32) + 0.5) * (1.0 / channels)
        basis.append(bernstein(position))
        target = sum(basis[channel][i] * consensus_ref[i] for i in range(3))
        turned[...] = ETA_STEP * (RHO_PENALTY * target - duals_ref[channel])
        base[channel] = jnp.zeros(base.shape[1:], F32)
        jones_cur[channel] = jnp.zeros(jones_cur.shape[1:], F32)
        for c in range(8):
            base[channel, c, :, 0:stations] = turned[:, c, :].T
            jones_cur[channel, c, :, 0:stations] = jones_ref[channel, :, c, :].T

    def divide(channel):
        high, low = split(jones_cur[channel].reshape(rows, GROUP))
        jones_split[channel, :, 0:GROUP] = high
        jones_split[channel, :, GROUP : 2 * GROUP] = low

    for channel in range(own):
        divide(channel)

    def coherency(channel, group, comp, first):
        if isinstance(group, int) and group == full:
            return coh_tail[channel, comp, first : first + 16, :].astype(F32)
        lanes = pl.ds(pl.multiple_of(group * GROUP, GROUP), GROUP)
        return coh_ref[channel, comp, first : first + 16, lanes].astype(F32)

    def gather(channel, group):
        both_now[channel][...] = jnp.dot(jones_split[channel], gather_hot[group], preferred_element_type=F32)

    def scatter_part(channel, group, side):
        lanes = slice(2 * side * GROUP, 2 * (side + 1) * GROUP)
        update_now[channel][...] += lax.dot_general(
            grad_parts[channel][:, lanes], spread_hot[group, :, lanes], (((1,), (1,)), ((), ())),
            preferred_element_type=F32,
        )

    def scatter(channel, group):
        for side in range(2):
            scatter_part(channel, group, side)

    def visit(channel, group, factor, between=(None, None, None)):
        both, propagated_ref, parts = both_now[channel], propagated_now[channel], grad_parts[channel]
        total = None
        for first_row in range(0, dirs, 16):
            wide = [coherency(channel, group, c, first_row) for c in range(8)]
            for upper in range(2):
                at = [slice(c * dirs + first_row + 8 * upper, c * dirs + first_row + 8 * upper + 8) for c in range(8)]
                source = [w[8 * upper : 8 * upper + 8] for w in wide]
                first = [both[at[c], 0:GROUP] for c in range(8)]
                propagated = product(first, source)
                for c in range(8):
                    propagated_ref[at[c], :] = propagated[c]
                second = [both[at[c], GROUP : 2 * GROUP] for c in range(8)]
                model = product_adjoint(propagated, second)
                total = model if total is None else [t + m for t, m in zip(total, model)]
        if between[0]:
            between[0]()
        lanes = pl.ds(pl.multiple_of(group * GROUP, GROUP), GROUP)
        residual = []
        for c in range(8):
            observed = vis_pad[channel, c : c + 1, lanes]
            value = (observed - jnp.sum(total[c], axis=0, keepdims=True)) * factor
            residual.append(jnp.broadcast_to(value, (16, GROUP)))
        place = [slice(n * GROUP, (n + 1) * GROUP) for n in range(4)]
        for first_row in range(0, dirs, 16):
            at = [slice(c * dirs + first_row, c * dirs + first_row + 16) for c in range(8)]
            source = [coherency(channel, group, c, first_row) for c in range(8)]
            second = [both[at[c], GROUP : 2 * GROUP] for c in range(8)]
            conjugated = product_adjoint(second, source)
            for c, value in enumerate(product_terms(residual, conjugated)):
                parts[at[c], place[0]], parts[at[c], place[1]] = split(value)
            propagated = [propagated_ref[at[c], :] for c in range(8)]
            for c, value in enumerate(adjoint_product_terms(residual, propagated)):
                parts[at[c], place[2]], parts[at[c], place[3]] = split(value)
            if between[1] and first_row == dirs // 2 - 16:
                between[1]()
        if between[2]:
            between[2]()

    factors = [counts_ref[channel].astype(F32) * (2.0 * ETA_STEP / SAMPLES) for channel in range(own)]

    def step(_, carry):
        for channel in range(own):
            update_now[channel][...] = jnp.zeros((rows, GROUP), F32)
        grad_parts[1][...] = jnp.zeros(grad_parts[1].shape, BF16)
        gather(0, 0)

        def sweep(group, carry):
            before = jnp.maximum(group - 1, 0)
            visit(0, group, factors[0], [
                lambda: gather(1, group), lambda: scatter_part(1, before, 0), lambda: scatter_part(1, before, 1)
            ])
            visit(1, group, factors[1], [
                lambda: scatter_part(0, group, 0), lambda: scatter_part(0, group, 1), lambda: gather(0, group + 1)
            ])
            return carry

        lax.fori_loop(0, groups - 1, sweep, 0)
        last = groups - 1
        visit(0, last, factors[0])
        gather(1, last)
        scatter(1, last - 1)
        visit(1, last, factors[1])
        scatter(0, last)
        scatter(1, last)
        for channel in range(own):
            update = update_now[channel][...].reshape(8, dirs, GROUP)
            jones_cur[channel] = (1.0 - ETA_STEP * RHO_PENALTY) * jones_cur[channel] + base[channel] + update
            divide(channel)
        return carry

    lax.fori_loop(0, STEPS, step, 0)

    for channel in range(own):
        for c in range(8):
            jones_out[channel, :, c, :] = jones_cur[channel, c].T[0:stations]
    near = stations // 2
    joined = [jones_out[channel] + duals_ref[channel] * (1.0 / RHO_PENALTY) for channel in range(own)]
    for i in range(3):
        value = sum(basis[channel][i] * joined[channel] for channel in range(own))
        sums_out[0:near, i] = jnp.concatenate([value[0:near], value[near : 2 * near]], axis=2)
        sums_out[near, i] = jnp.zeros((8, GROUP), F32)


def descend(channels, blocks, pairs, counts, jones, duals, consensus, visibilities, coherencies):
    own, stations, _, dirs = jones.shape
    count = pairs.shape[1]
    groups = -(-count // GROUP)
    lanes = groups * GROUP
    rows = 8 * dirs
    vmem = pl.BlockSpec(memory_space=pltpu.VMEM)
    smem = pl.BlockSpec(memory_space=pltpu.SMEM)
    return pl.pallas_call(
        functools.partial(descend_kernel, channels, blocks),
        out_shape=(
            jax.ShapeDtypeStruct(jones.shape, F32),
            jax.ShapeDtypeStruct((stations // 2 + 1, 3, 8, GROUP), F32),
        ),
        in_specs=[vmem, smem, vmem, vmem, vmem, vmem, vmem],
        out_specs=(vmem, vmem),
        scratch_shapes=[
            pltpu.VMEM((8, lanes), jnp.int32),
            pltpu.VMEM((own, 8, lanes), F32),
            pltpu.VMEM((own, 8, dirs, GROUP), BF16),
            pltpu.VMEM((groups, 2 * GROUP, 2 * GROUP), BF16),
            pltpu.VMEM((groups, GROUP, 4 * GROUP), BF16),
            pltpu.VMEM((own, 8, dirs, GROUP), F32),
            pltpu.VMEM((own, rows, 2 * GROUP), BF16),
            pltpu.VMEM((own, 8, dirs, GROUP), F32),
            pltpu.VMEM((stations, 8, dirs), F32),
            [pltpu.VMEM((rows, 2 * GROUP), F32)] * own,
            [pltpu.VMEM((rows, GROUP), F32)] * own,
            [pltpu.VMEM((rows, 4 * GROUP), BF16)] * own,
            [pltpu.VMEM((rows, GROUP), F32)] * own,
        ],
        compiler_params=pltpu.CompilerParams(vmem_limit_bytes=56 * 2**20),
        name="descend",
    )(pairs, counts, jones, duals, consensus, visibilities, coherencies)


def agree_kernel(
    channels, blocks, inverse, s_ref, jones_ref, duals_ref, consensus_out, duals_out,
    recv_core, mid, recv_plane, recv_col, full, s1, r1, s2, r2, s3, r3, s4, r4, s5, r5,
):
    z = lax.axis_index("grp"); chan = lax.axis_index("chan")
    core = chan % 2; u = chan // 2; x = u // SIDE; y = u % SIDE
    other = 1 - core
    def peer(dx, dy):
        return ((x + dx) % SIDE) * SIDE + (y + dy) % SIDE
    steps = sorted([(dx, dy) for dx in range(SIDE) for dy in range(SIDE) if dx or dy], key=lambda s: -(min(s[0],4-s[0])+min(s[1],4-s[1])))
    def back(dx, dy):
        return ((x - dx + SIDE) % SIDE) * SIDE + (y - dy + SIDE) % SIDE
    def dev(uu, cc): return {"grp": z, "chan": uu * 2 + cc}
    barrier = pltpu.get_barrier_semaphore()
    pl.semaphore_signal(barrier, inc=1, device_id=dev(u, other), device_id_type=MESH)
    for dx, dy in steps:
        pl.semaphore_signal(barrier, inc=1, device_id=dev(peer(dx, dy), core), device_id_type=MESH)
    for dz in range(1, SIDE):
        pl.semaphore_signal(barrier, inc=1, device_id={"grp": (z + dz) % SIDE, "chan": chan}, device_id_type=MESH)
    pl.semaphore_wait(barrier, 1 + len(steps) + SIDE - 1)
    order = steps + [(0, 0)]
    def rc(src, dst, ss, rs, d):
        return pltpu.make_async_remote_copy(src_ref=src, dst_ref=dst, send_sem=ss, recv_sem=rs, device_id=d, device_id_type=MESH)
    c1 = []
    for n, (dx, dy) in enumerate(order):
        c = rc(s_ref.at[other * 16 + peer(dx, dy)], recv_core.at[n], s1.at[n], r1.at[n], dev(u, other))
        c.start(); c1.append(c)
    c2 = []
    for n, (dx, dy) in enumerate(order):
        c1[n].wait_recv()
        mid[n] = s_ref[core * 16 + peer(dx, dy)] + recv_core[n]
        if n < 15:
            c = rc(mid.at[n], recv_plane.at[n], s2.at[n], r2.at[n], dev(peer(dx, dy), core))
            c.start(); c2.append(c)
    total = mid[15]
    for n in range(15):
        c2[n].wait_recv()
        total = total + recv_plane[n]
    recv_col[z] = total
    c3 = []
    for dz in range(1, SIDE):
        c = rc(recv_col.at[z], recv_col.at[z], s3.at[dz], r3.at[dz], {"grp": (z + dz) % SIDE, "chan": chan})
        c.start(); c3.append(c)
    for c in c3: c.wait_recv()
    total = recv_col[0] + recv_col[1] + recv_col[2] + recv_col[3]
    mine = core * 16 + u
    for i in range(3):
        full[mine, i] = sum(inverse[i][j] * total[j] for j in range(3))
    c4 = []
    for n, (dx, dy) in enumerate(steps):
        c = rc(full.at[mine], full.at[mine], s4.at[n], r4.at[n], dev(peer(dx, dy), core))
        c.start(); c4.append(c)
    c5 = []
    c = rc(full.at[mine], full.at[mine], s5.at[15], r5.at[15], dev(u, other))
    c.start(); c5.append(c)
    for n, (dx, dy) in reversed(list(enumerate(steps))):
        c4[n].wait_recv()
        unit = core * 16 + back(dx, dy)
        c = rc(full.at[unit], full.at[unit], s5.at[n], r5.at[n], dev(u, other))
        c.start(); c5.append(c)
    for c in c5: c.wait_recv()
    for c in c1 + c2 + c3 + c4 + c5: c.wait_send()
    own, stations, _, dirs = jones_ref.shape
    near = stations // 2
    for i in range(3):
        consensus_out[i, 0:near] = full[0:near, i, :, 0:dirs]
        consensus_out[i, near : 2 * near] = full[0:near, i, :, dirs : 2 * dirs]
    offset = (z * blocks + chan) * own
    for channel in range(own):
        basis = bernstein(((offset + channel).astype(F32) + 0.5) * (1.0 / channels))
        smooth = sum(basis[i] * consensus_out[i] for i in range(3))
        duals_out[channel] = duals_ref[channel] + RHO_PENALTY * (jones_ref[channel] - smooth)


def agree(channels, blocks, sums, jones, duals):
    inverse = [[float(v) for v in row] for row in gram_inverse(channels).astype(np.float32)]
    vmem = pl.BlockSpec(memory_space=pltpu.VMEM)
    unit = sums.shape[1:]
    dma = pltpu.SemaphoreType.DMA
    return pl.pallas_call(
        functools.partial(agree_kernel, channels, blocks, inverse),
        out_shape=(jax.ShapeDtypeStruct((3,) + jones.shape[1:], F32), jax.ShapeDtypeStruct(duals.shape, F32)),
        in_specs=[vmem] * 3,
        out_specs=(vmem, vmem),
        scratch_shapes=[pltpu.VMEM((SIDE * SIDE,) + unit, F32)] * 3
        + [pltpu.VMEM((SIDE,) + unit, F32), pltpu.VMEM((2 * SIDE * SIDE,) + unit, F32)]
        + [dma((SIDE * SIDE,))] * 4
        + [dma((SIDE,))] * 2
        + [dma((SIDE * SIDE,))] * 4,
        compiler_params=pltpu.CompilerParams(
            collective_id=0, has_side_effects=True, vmem_limit_bytes=32 * 2**20
        ),
        name="agree",
    )(sums, jones, duals)


def shards(jones_start, duals_start, consensus_start, visibilities, coherencies, pairs, counts):
    blocks = lax.axis_size("chan")
    channels = jones_start.shape[0] * lax.axis_size("grp") * blocks
    jones, duals, consensus = (jnp.transpose(a, (0, 3, 1, 2)) for a in (jones_start, duals_start, consensus_start))
    jones, sums = descend(channels, blocks, pairs, counts, jones, duals, consensus, visibilities, coherencies)
    consensus, duals = agree(channels, blocks, sums, jones, duals)
    return tuple(jnp.transpose(a, (0, 2, 3, 1)) for a in (jones, duals, consensus))


def solution(mesh):
    in_specs = (
        P(("grp", "chan"), None, None, None),
        P(("grp", "chan"), None, None, None),
        P(),
        P(("grp", "chan"), None, None),
        P(("grp", "chan"), None, None, None),
        P(),
        P(("grp", "chan")),
    )
    out_specs = (P(("grp", "chan"), None, None, None), P(("grp", "chan"), None, None, None), P())
    return jax.shard_map(shards, mesh=mesh, in_specs=in_specs, out_specs=out_specs, check_vma=False)
```

time: 221 us -> 70.6 us (0.32)
  waiting for transfers between devices: 148 us -> 0 us
  Pallas kernels: 46.7 us -> 66 us
  between operations: 14.1 us -> 0.65 us
  local copies, waits for them, and re-layouts: 10.8 us -> 3.69 us
    psum x1 -> x0, waiting for transfers between devices: 148 us -> none  [shards(): sums = lax.psum(local_sums, ('grp', 'chan'))]
    pallas_call x0 -> x1, Pallas kernels: none -> 26.3 us  [agree(): pl.pallas_call(functools.partial(agree_kernel, channels, blocks, inverse)...]
    unnamed x10 -> x8, local copies, waits for them, and re-layouts: 10.8 us -> 3.69 us
    pallas_call x1, Pallas kernels: 46.7 us -> 39.8 us  [descend(): pl.pallas_call(functools.partial(descend_kernel, channels, blocks), out_s...]
  transfers between devices with their start and end apart: 1 -> 0, of which waited for: 1 -> 0; matrix products, arithmetic and copies ran while one was open for 1% -> 0% of each run, Pallas kernels for 0% -> 0%
where the time goes in v2:
time: 70.6 us; the launch traced here: 70.4 us
  Pallas kernels  66 us (93%)
  local copies, waits for them, and re-layouts  3.69 us (5%)
    pallas_call x1, Pallas kernels, descend(): pl.pallas_call(functools.partial(descend_kernel, channels, blocks), out_s...  39.8 us
    pallas_call x1, Pallas kernels, agree(): pl.pallas_call(functools.partial(agree_kernel, channels, blocks, inverse)...  26.3 us
    unnamed x8, local copies, waits for them, and re-layouts  3.69 us

profile of v2, /device:TPU:1, one launch (start us, length us, event | category | flops | bytes accessed | tf_op | source)
XLA Modules:
  0.0 70.4 jit_solution(1669781245757836726)
XLA Ops:
  0.6 0.0 copy-start
  0.6 39.8 %descend.1 = (f32[2,62,8,64]{3,2,1,0:T(8,128)}, f32[32,3,8,128]{3,2,1,0:T(8,128)}) custom-call(s32[2,1891]{1,0:T(2,128)} %pairs_ref.1, s32[2]{0:T(128)} %counts_ref.1, f32[2,62,8,64]{3,2,1,0:T(8,128)} %bitcast.12, f32[2,62,8,64]{3,2,1,0:T(8,128)} %bitcast.6, f32[3,62,8,64]{3,2,1,0:T(8,128)} %bitcast.11, f32[2,8,1891]{2,1,0:T(8,128)} %vis_ref.1, ...), custom_call_target="tpu_custom_call" | custom-call | tf_op jit(solution)/shard_map/descend/pallas_call | solution.py:251
  40.4 0.0 copy-done
  40.4 0.0 copy-start.1
  40.4 1.0 %copy-done.1 = f32[2,62,8,64]{3,2,1,0:T(8,128)S(1)} copy-done((f32[2,62,8,64]{3,2,1,0:T(8,128)S(1)}, f32[2,62,8,64]{3,2,1,0:T(8,128)}, u32[]{:S(2)}) %copy-start.1) | copy-done | bytes 253976
  41.4 0.0 copy-start.2
  41.4 1.0 %copy-done.2 = f32[32,3,8,128]{3,2,1,0:T(8,128)S(1)} copy-done((f32[32,3,8,128]{3,2,1,0:T(8,128)S(1)}, f32[32,3,8,128]{3,2,1,0:T(8,128)}, u32[]{:S(2)}) %copy-start.2) | copy-done | bytes 393240
  42.4 26.3 %agree.1 = (f32[3,62,8,64]{3,2,1,0:T(8,128)S(1)}, f32[2,62,8,64]{3,2,1,0:T(8,128)S(1)}) custom-call(f32[32,3,8,128]{3,2,1,0:T(8,128)S(1)} %copy-done.2, f32[2,62,8,64]{3,2,1,0:T(8,128)S(1)} %copy-done.1, f32[2,62,8,64]{3,2,1,0:T(8,128)S(1)} %bitcast.7), custom_call_target="tpu_custom_call" | custom-call | tf_op jit(solution)/shard_map/agree/pallas_call | solution.py:358
  68.7 0.8 %copy.12 = f32[2,8,64,62]{2,1,3,0:T(8,128)} copy(f32[2,8,64,62]{2,1,3,0:T(8,128)S(1)} %bitcast.9) | data formatting | bytes 507904
  69.5 0.9 %copy.13 = f32[3,8,64,62]{2,1,3,0:T(8,128)} copy(f32[3,8,64,62]{2,1,3,0:T(8,128)S(1)} %bitcast.8) | data formatting | bytes 761856
Async XLA Ops:
  0.6 39.8 %copy-start = (f32[2,8,64,62]{2,1,3,0:T(8,128)S(1)}, f32[2,8,64,62]{2,1,3,0:T(8,128)}, u32[]{:S(2)}) copy-start(f32[2,8,64,62]{2,1,3,0:T(8,128)} %param.8) | copy-start | bytes 761860
  40.4 1.0 %copy-start.1 = (f32[2,62,8,64]{3,2,1,0:T(8,128)S(1)}, f32[2,62,8,64]{3,2,1,0:T(8,128)}, u32[]{:S(2)}) copy-start(f32[2,62,8,64]{3,2,1,0:T(8,128)} %get-tuple-element.7.jones_ref) | copy-start | bytes 761860
  41.4 1.0 %copy-start.2 = (f32[32,3,8,128]{3,2,1,0:T(8,128)S(1)}, f32[32,3,8,128]{3,2,1,0:T(8,128)}, u32[]{:S(2)}) copy-start(f32[32,3,8,128]{3,2,1,0:T(8,128)} %get-tuple-element.8.s_ref) | copy-start | bytes 1179652

commit v3 on v2

--- a/solution.py
+++ b/solution.py
@@ -86,18 +86,39 @@
     return high, low
 
 
+def greet(wait):
+    barrier = pltpu.get_barrier_semaphore()
+    z, chan = lax.axis_index("grp"), lax.axis_index("chan")
+    core, u = chan % 2, chan // 2
+    if wait:
+        pl.semaphore_wait(barrier, 1 + SIDE * SIDE - 1 + SIDE - 1)
+        return
+    pl.semaphore_signal(barrier, inc=1, device_id={"grp": z, "chan": u * 2 + 1 - core}, device_id_type=MESH)
+    for dx in range(SIDE):
+        for dy in range(SIDE):
+            if dx or dy:
+                there = ((u // SIDE + dx) % SIDE) * SIDE + (u % SIDE + dy) % SIDE
+                pl.semaphore_signal(
+                    barrier, inc=1, device_id={"grp": z, "chan": there * 2 + core}, device_id_type=MESH
+                )
+    for dz in range(1, SIDE):
+        pl.semaphore_signal(barrier, inc=1, device_id={"grp": (z + dz) % SIDE, "chan": chan}, device_id_type=MESH)
+
+
 def descend_kernel(
-    channels, blocks, pairs_ref, counts_ref, jones_ref, duals_ref, consensus_ref, vis_ref, coh_ref,
-    jones_out, sums_out,
-    pairs_pad, vis_pad, coh_tail, gather_hot, spread_hot, jones_cur, jones_split, base, turned, both_now,
-    propagated_now, grad_parts, update_now,
+    channels, blocks, inverse, pairs_ref, counts_ref, jones_ref, duals_ref, consensus_ref, vis_ref, coh_ref,
+    jones_out, duals_out, consensus_out, sums_out,
+    pairs_pad, vis_pad, coh_tail, spread_hot, jones_cur, base, turned, both_now,
+    propagated_now, grad_parts, update_now, *links,
 ):
     own, stations, _, dirs = jones_ref.shape
     count = pairs_ref.shape[1]
-    groups = gather_hot.shape[0]
+    groups = spread_hot.shape[0]
     full = count // GROUP
     rows = 8 * dirs
     offset = (lax.axis_index("grp") * blocks + lax.axis_index("chan")) * own
+
+    greet(False)
 
     pairs_pad[...] = jnp.full(pairs_pad.shape, -1, jnp.int32)
     pairs_pad[0:2, 0:count] = pairs_ref[...]
@@ -112,7 +133,6 @@
             row = pairs_pad[side : side + 1, group * GROUP : (group + 1) * GROUP]
             hot = jnp.where(ids == row, 1.0, 0.0).astype(BF16)
             for part in range(2):
-                gather_hot[group, part * GROUP : (part + 1) * GROUP, side * GROUP : (side + 1) * GROUP] = hot
                 where = (2 * side + part) * GROUP
                 spread_hot[group, :, where : where + GROUP] = hot
 
@@ -128,22 +148,11 @@
             base[channel, c, :, 0:stations] = turned[:, c, :].T
             jones_cur[channel, c, :, 0:stations] = jones_ref[channel, :, c, :].T
 
-    def divide(channel):
-        high, low = split(jones_cur[channel].reshape(rows, GROUP))
-        jones_split[channel, :, 0:GROUP] = high
-        jones_split[channel, :, GROUP : 2 * GROUP] = low
-
-    for channel in range(own):
-        divide(channel)
-
     def coherency(channel, group, comp, first):
         if isinstance(group, int) and group == full:
             return coh_tail[channel, comp, first : first + 16, :].astype(F32)
         lanes = pl.ds(pl.multiple_of(group * GROUP, GROUP), GROUP)
         return coh_ref[channel, comp, first : first + 16, lanes].astype(F32)
-
-    def gather(channel, group):
-        both_now[channel][...] = jnp.dot(jones_split[channel], gather_hot[group], preferred_element_type=F32)
 
     def scatter_part(channel, group, side):
         lanes = slice(2 * side * GROUP, 2 * (side + 1) * GROUP)
@@ -156,8 +165,22 @@
         for side in range(2):
             scatter_part(channel, group, side)
 
-    def visit(channel, group, factor, between=(None, None, None)):
+    def stations_of(side, group):
+        lanes = pl.ds(group * GROUP if isinstance(group, int) else pl.multiple_of(group * GROUP, GROUP), GROUP)
+        return jnp.broadcast_to(jnp.maximum(pairs_pad[side : side + 1, lanes], 0), (8, GROUP))
+
+    def fetch(channel, which, first_row, depth):
+        for row in range(first_row, first_row + depth, 8):
+            for c in range(8):
+                table = jones_cur[channel, c, row : row + 8, :]
+                for side in range(2):
+                    both_now[channel][c * dirs + row : c * dirs + row + 8, side * GROUP : (side + 1) * GROUP] = (
+                        jnp.take_along_axis(table, which[side], axis=1)
+                    )
+
+    def visit(channel, group, factor, following=None, between=(None, None, None)):
         both, propagated_ref, parts = both_now[channel], propagated_now[channel], grad_parts[channel]
+        lanes = pl.ds(group * GROUP if isinstance(group, int) else pl.multiple_of(group * GROUP, GROUP), GROUP)
         total = None
         for first_row in range(0, dirs, 16):
             wide = [coherency(channel, group, c, first_row) for c in range(8)]
@@ -180,6 +203,8 @@
             value = (observed - jnp.sum(total[c], axis=0, keepdims=True)) * factor
             residual.append(jnp.broadcast_to(value, (16, GROUP)))
         place = [slice(n * GROUP, (n + 1) * GROUP) for n in range(4)]
+        if following:
+            which = [stations_of(side, following[1]) for side in range(2)]
         for first_row in range(0, dirs, 16):
             at = [slice(c * dirs + first_row, c * dirs + first_row + 16) for c in range(8)]
             source = [coherency(channel, group, c, first_row) for c in range(8)]
@@ -190,6 +215,8 @@
             propagated = [propagated_ref[at[c], :] for c in range(8)]
             for c, value in enumerate(adjoint_product_terms(residual, propagated)):
                 parts[at[c], place[2]], parts[at[c], place[3]] = split(value)
+            if following:
+                fetch(following[0], which, first_row, 16)
             if between[1] and first_row == dirs // 2 - 16:
                 between[1]()
         if between[2]:
@@ -201,22 +228,22 @@
         for channel in range(own):
             update_now[channel][...] = jnp.zeros((rows, GROUP), F32)
         grad_parts[1][...] = jnp.zeros(grad_parts[1].shape, BF16)
-        gather(0, 0)
+
+        fetch(0, [stations_of(side, 0) for side in range(2)], 0, dirs)
 
         def sweep(group, carry):
             before = jnp.maximum(group - 1, 0)
-            visit(0, group, factors[0], [
-                lambda: gather(1, group), lambda: scatter_part(1, before, 0), lambda: scatter_part(1, before, 1)
+            visit(0, group, factors[0], (1, group), [
+                None, None, lambda: scatter(1, before)
             ])
-            visit(1, group, factors[1], [
-                lambda: scatter_part(0, group, 0), lambda: scatter_part(0, group, 1), lambda: gather(0, group + 1)
+            visit(1, group, factors[1], (0, group + 1), [
+                None, None, lambda: scatter(0, group)
             ])
             return carry
 
         lax.fori_loop(0, groups - 1, sweep, 0)
         last = groups - 1
-        visit(0, last, factors[0])
-        gather(1, last)
+        visit(0, last, factors[0], (1, last))
         scatter(1, last - 1)
         visit(1, last, factors[1])
         scatter(0, last)
@@ -224,7 +251,6 @@
         for channel in range(own):
             update = update_now[channel][...].reshape(8, dirs, GROUP)
             jones_cur[channel] = (1.0 - ETA_STEP * RHO_PENALTY) * jones_cur[channel] + base[channel] + update
-            divide(channel)
         return carry
 
     lax.fori_loop(0, STEPS, step, 0)
@@ -238,6 +264,7 @@
         value = sum(basis[channel][i] * joined[channel] for channel in range(own))
         sums_out[0:near, i] = jnp.concatenate([value[0:near], value[near : 2 * near]], axis=2)
         sums_out[near, i] = jnp.zeros((8, GROUP), F32)
+    agree_kernel(channels, blocks, inverse, sums_out, jones_out, duals_ref, consensus_out, duals_out, *links)
 
 
 def descend(channels, blocks, pairs, counts, jones, duals, consensus, visibilities, coherencies):
@@ -246,32 +273,39 @@
     groups = -(-count // GROUP)
     lanes = groups * GROUP
     rows = 8 * dirs
+    unit = (3, 8, GROUP)
+    planes = SIDE * SIDE
+    dma = pltpu.SemaphoreType.DMA
+    inverse = [[float(v) for v in row] for row in gram_inverse(channels).astype(np.float32)]
     vmem = pl.BlockSpec(memory_space=pltpu.VMEM)
     smem = pl.BlockSpec(memory_space=pltpu.SMEM)
     return pl.pallas_call(
-        functools.partial(descend_kernel, channels, blocks),
-        out_shape=(
-            jax.ShapeDtypeStruct(jones.shape, F32),
-            jax.ShapeDtypeStruct((stations // 2 + 1, 3, 8, GROUP), F32),
-        ),
+        functools.partial(descend_kernel, channels, blocks, inverse),
+        out_shape=tuple(jax.ShapeDtypeStruct(a.shape, F32) for a in (jones, duals, consensus)),
         in_specs=[vmem, smem, vmem, vmem, vmem, vmem, vmem],
-        out_specs=(vmem, vmem),
+        out_specs=(vmem, vmem, vmem),
         scratch_shapes=[
+            pltpu.VMEM((stations // 2 + 1,) + unit, F32),
             pltpu.VMEM((8, lanes), jnp.int32),
             pltpu.VMEM((own, 8, lanes), F32),
             pltpu.VMEM((own, 8, dirs, GROUP), BF16),
-            pltpu.VMEM((groups, 2 * GROUP, 2 * GROUP), BF16),
             pltpu.VMEM((groups, GROUP, 4 * GROUP), BF16),
             pltpu.VMEM((own, 8, dirs, GROUP), F32),
-            pltpu.VMEM((own, rows, 2 * GROUP), BF16),
             pltpu.VMEM((own, 8, dirs, GROUP), F32),
             pltpu.VMEM((stations, 8, dirs), F32),
             [pltpu.VMEM((rows, 2 * GROUP), F32)] * own,
             [pltpu.VMEM((rows, GROUP), F32)] * own,
             [pltpu.VMEM((rows, 4 * GROUP), BF16)] * own,
             [pltpu.VMEM((rows, GROUP), F32)] * own,
-        ],
-        compiler_params=pltpu.CompilerParams(vmem_limit_bytes=56 * 2**20),
+        ]
+        + [pltpu.VMEM((planes,) + unit, F32)] * 3
+        + [pltpu.VMEM((SIDE,) + unit, F32), pltpu.VMEM((2 * planes,) + unit, F32)]
+        + [dma((planes,))] * 4
+        + [dma((SIDE,))] * 2
+        + [dma((planes,))] * 4,
+        compiler_params=pltpu.CompilerParams(
+            collective_id=0, has_side_effects=True, vmem_limit_bytes=28 * 2**20
+        ),
         name="descend",
     )(pairs, counts, jones, duals, consensus, visibilities, coherencies)
 
@@ -289,13 +323,7 @@
     def back(dx, dy):
         return ((x - dx + SIDE) % SIDE) * SIDE + (y - dy + SIDE) % SIDE
     def dev(uu, cc): return {"grp": z, "chan": uu * 2 + cc}
-    barrier = pltpu.get_barrier_semaphore()
-    pl.semaphore_signal(barrier, inc=1, device_id=dev(u, other), device_id_type=MESH)
-    for dx, dy in steps:
-        pl.semaphore_signal(barrier, inc=1, device_id=dev(peer(dx, dy), core), device_id_type=MESH)
-    for dz in range(1, SIDE):
-        pl.semaphore_signal(barrier, inc=1, device_id={"grp": (z + dz) % SIDE, "chan": chan}, device_id_type=MESH)
-    pl.semaphore_wait(barrier, 1 + len(steps) + SIDE - 1)
+    greet(True)
     order = steps + [(0, 0)]
     def rc(src, dst, ss, rs, d):
         return pltpu.make_async_remote_copy(src_ref=src, dst_ref=dst, send_sem=ss, recv_sem=rs, device_id=d, device_id_type=MESH)
@@ -350,35 +378,12 @@
         duals_out[channel] = duals_ref[channel] + RHO_PENALTY * (jones_ref[channel] - smooth)
 
 
-def agree(channels, blocks, sums, jones, duals):
-    inverse = [[float(v) for v in row] for row in gram_inverse(channels).astype(np.float32)]
-    vmem = pl.BlockSpec(memory_space=pltpu.VMEM)
-    unit = sums.shape[1:]
-    dma = pltpu.SemaphoreType.DMA
-    return pl.pallas_call(
-        functools.partial(agree_kernel, channels, blocks, inverse),
-        out_shape=(jax.ShapeDtypeStruct((3,) + jones.shape[1:], F32), jax.ShapeDtypeStruct(duals.shape, F32)),
-        in_specs=[vmem] * 3,
-        out_specs=(vmem, vmem),
-        scratch_shapes=[pltpu.VMEM((SIDE * SIDE,) + unit, F32)] * 3
-        + [pltpu.VMEM((SIDE,) + unit, F32), pltpu.VMEM((2 * SIDE * SIDE,) + unit, F32)]
-        + [dma((SIDE * SIDE,))] * 4
-        + [dma((SIDE,))] * 2
-        + [dma((SIDE * SIDE,))] * 4,
-        compiler_params=pltpu.CompilerParams(
-            collective_id=0, has_side_effects=True, vmem_limit_bytes=32 * 2**20
-        ),
-        name="agree",
-    )(sums, jones, duals)
-
-
 def shards(jones_start, duals_start, consensus_start, visibilities, coherencies, pairs, counts):
     blocks = lax.axis_size("chan")
     channels = jones_start.shape[0] * lax.axis_size("grp") * blocks
     jones, duals, consensus = (jnp.transpose(a, (0, 3, 1, 2)) for a in (jones_start, duals_start, consensus_start))
-    jones, sums = descend(channels, blocks, pairs, counts, jones, duals, consensus, visibilities, coherencies)
-    consensus, duals = agree(channels, blocks, sums, jones, duals)
-    return tuple(jnp.transpose(a, (0, 2, 3, 1)) for a in (jones, duals, consensus))
+    outs = descend(channels, blocks, pairs, counts, jones, duals, consensus, visibilities, coherencies)
+    return tuple(jnp.transpose(a, (0, 2, 3, 1)) for a in outs)
 
 
 def solution(mesh):

time: 70.6 us -> 65.8 us (0.932)
  Pallas kernels: 66 us -> 54.8 us
  local copies, waits for them, and re-layouts: 3.69 us -> 10 us
    pallas_call x2 -> x1, Pallas kernels: 66 us -> 54.8 us  [descend(): pl.pallas_call(functools.partial(descend_kernel, channels, blocks, invers...]
    unnamed x8 -> x17, local copies, waits for them, and re-layouts: 3.69 us -> 10 us
where the time goes in v3:
time: 65.8 us; the launch traced here: 65.5 us
  Pallas kernels  54.8 us (83%)
  local copies, waits for them, and re-layouts  10 us (15%)
  between operations  0.66 us (1%)
    pallas_call x1, Pallas kernels, descend(): pl.pallas_call(functools.partial(descend_kernel, channels, blocks, invers...  54.8 us
    unnamed x17, local copies, waits for them, and re-layouts  10 us

profile of v3, /device:TPU:1, one launch (start us, length us, event | category | flops | bytes accessed | tf_op | source)
XLA Modules:
  0.0 65.5 jit_solution(8220173640929482967)
XLA Ops:
  0.6 0.0 copy-start
  0.6 2.1 %copy-done = bf16[2,8,64,1891]{3,2,1,0:T(8,128)(2,1)S(1)} copy-done((bf16[2,8,64,1891]{3,2,1,0:T(8,128)(2,1)S(1)}, bf16[2,8,64,1891]{3,2,1,0:T(8,128)(2,1)}, u32[]{:S(2)}) %copy-start) | copy-done | bytes 3872792
  2.7 0.0 copy-start.1
  2.7 1.1 %copy-done.1 = f32[3,8,64,62]{2,1,3,0:T(8,128)S(1)} copy-done((f32[3,8,64,62]{2,1,3,0:T(8,128)S(1)}, f32[3,8,64,62]{2,1,3,0:T(8,128)}, u32[]{:S(2)}) %copy-start.1) | copy-done | bytes 380952
  3.9 0.0 copy-start.2
  3.9 1.0 %copy-done.2 = f32[2,8,64,62]{2,1,3,0:T(8,128)S(1)} copy-done((f32[2,8,64,62]{2,1,3,0:T(8,128)S(1)}, f32[2,8,64,62]{2,1,3,0:T(8,128)}, u32[]{:S(2)}) %copy-start.2) | copy-done | bytes 253976
  4.9 0.0 copy-start.3
  4.9 1.0 %copy-done.3 = f32[2,8,64,62]{2,1,3,0:T(8,128)S(1)} copy-done((f32[2,8,64,62]{2,1,3,0:T(8,128)S(1)}, f32[2,8,64,62]{2,1,3,0:T(8,128)}, u32[]{:S(2)}) %copy-start.3) | copy-done | bytes 253976
  5.9 0.0 copy-start.4
  5.9 0.9 %copy-done.4 = f32[2,8,1891]{2,1,0:T(8,128)S(1)} copy-done((f32[2,8,1891]{2,1,0:T(8,128)S(1)}, f32[2,8,1891]{2,1,0:T(8,128)}, u32[]{:S(2)}) %copy-start.4) | copy-done | bytes 121048
  6.8 0.0 copy-start.5
  6.8 0.7 %copy-done.5 = s32[2,1891]{1,0:T(2,128)S(1)} copy-done((s32[2,1891]{1,0:T(2,128)S(1)}, s32[2,1891]{1,0:T(2,128)}, u32[]{:S(2)}) %copy-start.5) | copy-done | bytes 15152
  7.6 0.0 copy-start.6
  7.6 0.7 copy-done.6
  8.2 54.8 %descend.1 = (f32[2,62,8,64]{3,2,1,0:T(8,128)S(1)}, f32[2,62,8,64]{3,2,1,0:T(8,128)S(1)}, f32[3,62,8,64]{3,2,1,0:T(8,128)S(1)}) custom-call(s32[2,1891]{1,0:T(2,128)S(1)} %copy-done.5, s32[2]{0:T(128)S(1)} %copy-done.6, f32[2,62,8,64]{3,2,1,0:T(8,128)S(1)} %bitcast.10, f32[2,62,8,64]{3,2,1,0:T(8,128)S(1)} %bitcast.11, f32[3,62,8,64]{3,2,1,0:T(8,128)S(1)} %bitcast.7, ...), custom_call_target="tpu_custom_call" | custom-call | tf_op jit(solution)/shard_map/descend/pallas_call | solution.py:282
  63.0 0.8 %copy.13 = f32[2,8,64,62]{2,1,3,0:T(8,128)} copy(f32[2,8,64,62]{2,1,3,0:T(8,128)S(1)} %bitcast.9) | data formatting | bytes 507904
  63.8 0.8 %copy.14 = f32[2,8,64,62]{2,1,3,0:T(8,128)} copy(f32[2,8,64,62]{2,1,3,0:T(8,128)S(1)} %bitcast.8) | data formatting | bytes 507904
  64.6 0.9 %copy.15 = f32[3,8,64,62]{2,1,3,0:T(8,128)} copy(f32[3,8,64,62]{2,1,3,0:T(8,128)S(1)} %bitcast.6) | data formatting | bytes 761856
Async XLA Ops:
  0.6 2.1 %copy-start = (bf16[2,8,64,1891]{3,2,1,0:T(8,128)(2,1)S(1)}, bf16[2,8,64,1891]{3,2,1,0:T(8,128)(2,1)}, u32[]{:S(2)}) copy-start(bf16[2,8,64,1891]{3,2,1,0:T(8,128)(2,1)} %coh_ref.1) | copy-start | bytes 11618308
  2.7 1.1 %copy-start.1 = (f32[3,8,64,62]{2,1,3,0:T(8,128)S(1)}, f32[3,8,64,62]{2,1,3,0:T(8,128)}, u32[]{:S(2)}) copy-start(f32[3,8,64,62]{2,1,3,0:T(8,128)} %param.9) | copy-start | bytes 1142788
  3.9 1.0 %copy-start.2 = (f32[2,8,64,62]{2,1,3,0:T(8,128)S(1)}, f32[2,8,64,62]{2,1,3,0:T(8,128)}, u32[]{:S(2)}) copy-start(f32[2,8,64,62]{2,1,3,0:T(8,128)} %param.7) | copy-start | bytes 761860
  4.9 1.0 %copy-start.3 = (f32[2,8,64,62]{2,1,3,0:T(8,128)S(1)}, f32[2,8,64,62]{2,1,3,0:T(8,128)}, u32[]{:S(2)}) copy-start(f32[2,8,64,62]{2,1,3,0:T(8,128)} %param.8) | copy-start | bytes 761860
  5.9 0.9 %copy-start.4 = (f32[2,8,1891]{2,1,0:T(8,128)S(1)}, f32[2,8,1891]{2,1,0:T(8,128)}, u32[]{:S(2)}) copy-start(f32[2,8,1891]{2,1,0:T(8,128)} %vis_ref.1) | copy-start | bytes 363076
  6.8 0.7 %copy-start.5 = (s32[2,1891]{1,0:T(2,128)S(1)}, s32[2,1891]{1,0:T(2,128)}, u32[]{:S(2)}) copy-start(s32[2,1891]{1,0:T(2,128)} %pairs_ref.1) | copy-start | bytes 45388
  7.6 0.7 %copy-start.6 = (s32[2]{0:T(128)S(1)}, s32[2]{0:T(128)}, u32[]{:S(2)}) copy-start(s32[2]{0:T(128)} %counts_ref.1) | copy-start | bytes 28

commit v4 on v3

--- a/solution.py
+++ b/solution.py
@@ -35,49 +35,33 @@
     return np.stack(rows).T / np.sum(matrix[0] * rows[0])
 
 
-def product_terms(a, b):
-    for row in range(2):
-        for col in range(2):
-            lr, li = a[4 * row], a[4 * row + 1]
-            mr, mi = a[4 * row + 2], a[4 * row + 3]
-            br, bi = b[2 * col], b[2 * col + 1]
-            dr, di = b[4 + 2 * col], b[4 + 2 * col + 1]
-            yield ((lr * br - li * bi) + (mr * dr - mi * di))
-            yield ((lr * bi + li * br) + (mr * di + mi * dr))
-
-
-def product(a, b):
-    return list(product_terms(a, b))
-
-
-def product_adjoint_terms(a, b):
-    for row in range(2):
-        for col in range(2):
-            lr, li = a[4 * row], a[4 * row + 1]
-            mr, mi = a[4 * row + 2], a[4 * row + 3]
-            br, bi = b[4 * col], b[4 * col + 1]
-            dr, di = b[4 * col + 2], b[4 * col + 3]
-            yield ((lr * br + li * bi) + (mr * dr + mi * di))
-            yield ((li * br - lr * bi) + (mi * dr - mr * di))
-
-
-def product_adjoint(a, b):
-    return list(product_adjoint_terms(a, b))
-
-
-def adjoint_product_terms(a, b):
-    for row in range(2):
-        for col in range(2):
-            lr, li = a[2 * row], a[2 * row + 1]
-            mr, mi = a[4 + 2 * row], a[4 + 2 * row + 1]
-            br, bi = b[2 * col], b[2 * col + 1]
-            dr, di = b[4 + 2 * col], b[4 + 2 * col + 1]
-            yield ((lr * br + li * bi) + (mr * dr + mi * di))
-            yield ((lr * bi - li * br) + (mr * di - mi * dr))
-
-
-def adjoint_product(a, b):
-    return list(adjoint_product_terms(a, b))
+def triple(entry):
+    return entry[0], entry[1] - entry[0], entry[0] + entry[1]
+
+
+def total_of(values):
+    return functools.reduce(lambda former, latter: former + latter, values)
+
+
+def plain(factors):
+    first = total_of([a[2] * b[0] for a, b in factors])
+    return first - total_of([a[1] * b[2] for a, b in factors]), first + total_of([a[0] * b[1] for a, b in factors])
+
+
+def conjugated(factors):
+    return (
+        total_of([a[2] * b[0] for a, b in factors]),
+        total_of([a[1] * b[1] for a, b in factors]),
+        total_of([a[0] * b[2] for a, b in factors]),
+    )
+
+
+def entries(values):
+    return [(values[2 * n], values[2 * n + 1]) for n in range(4)]
+
+
+def with_sum(entry):
+    return entry[0], entry[1], entry[0] + entry[1]
 
 
 def split(value):
@@ -106,10 +90,11 @@
 
 
 def descend_kernel(
-    channels, blocks, inverse, pairs_ref, counts_ref, jones_ref, duals_ref, consensus_ref, vis_ref, coh_ref,
+    channels, blocks, inverse, pairs_in, counts_ref, jones_in, duals_in, consensus_in, vis_in, coh_in,
     jones_out, duals_out, consensus_out, sums_out,
     pairs_pad, vis_pad, coh_tail, spread_hot, jones_cur, base, turned, both_now,
-    propagated_now, grad_parts, update_now, *links,
+    propagated_now, turned_now, grad_parts, update_now, pairs_ref, jones_ref, duals_ref, consensus_ref, vis_ref, coh_ref,
+    arrived, *links,
 ):
     own, stations, _, dirs = jones_ref.shape
     count = pairs_ref.shape[1]
@@ -119,13 +104,17 @@
     offset = (lax.axis_index("grp") * blocks + lax.axis_index("chan")) * own
 
     greet(False)
+    inputs = [
+        (pairs_in, pairs_ref), (vis_in, vis_ref), (consensus_in, consensus_ref), (duals_in, duals_ref),
+        (jones_in, jones_ref), (coh_in, coh_ref),
+    ]
+    inputs = [pltpu.make_async_copy(a, b, arrived.at[n]) for n, (a, b) in enumerate(inputs)]
+    for copy in inputs:
+        copy.start()
 
     pairs_pad[...] = jnp.full(pairs_pad.shape, -1, jnp.int32)
+    inputs[0].wait()
     pairs_pad[0:2, 0:count] = pairs_ref[...]
-    vis_pad[...] = jnp.zeros(vis_pad.shape, F32)
-    vis_pad[:, :, 0:count] = vis_ref[...]
-    coh_tail[...] = jnp.zeros(coh_tail.shape, BF16)
-    coh_tail[:, :, :, 0 : count - full * GROUP] = coh_ref[:, :, :, full * GROUP : count]
 
     ids = lax.broadcasted_iota(jnp.int32, (GROUP, GROUP), 0)
     for group in range(groups):
@@ -136,17 +125,26 @@
                 where = (2 * side + part) * GROUP
                 spread_hot[group, :, where : where + GROUP] = hot
 
+    inputs[1].wait()
+    vis_pad[...] = jnp.zeros(vis_pad.shape, F32)
+    vis_pad[:, :, 0:count] = vis_ref[...]
+    for copy in inputs[2:5]:
+        copy.wait()
+
     basis = []
     for channel in range(own):
         position = ((offset + channel).astype(F32) + 0.5) * (1.0 / channels)
         basis.append(bernstein(position))
         target = sum(basis[channel][i] * consensus_ref[i] for i in range(3))
-        turned[...] = ETA_STEP * (RHO_PENALTY * target - duals_ref[channel])
+        turned[channel] = ETA_STEP * (RHO_PENALTY * target - duals_ref[channel])
         base[channel] = jnp.zeros(base.shape[1:], F32)
         jones_cur[channel] = jnp.zeros(jones_cur.shape[1:], F32)
         for c in range(8):
-            base[channel, c, :, 0:stations] = turned[:, c, :].T
             jones_cur[channel, c, :, 0:stations] = jones_ref[channel, :, c, :].T
+
+    def turn(channel):
+        for c in range(8):
+            base[channel, c, :, 0:stations] = turned[channel, :, c, :].T
 
     def coherency(channel, group, comp, first):
         if isinstance(group, int) and group == full:
@@ -179,42 +177,63 @@
                     )
 
     def visit(channel, group, factor, following=None, between=(None, None, None)):
-        both, propagated_ref, parts = both_now[channel], propagated_now[channel], grad_parts[channel]
+        both, propagated_ref, turned_ref = both_now[channel], propagated_now[channel], turned_now[channel]
+        parts = grad_parts[channel]
         lanes = pl.ds(group * GROUP if isinstance(group, int) else pl.multiple_of(group * GROUP, GROUP), GROUP)
         total = None
         for first_row in range(0, dirs, 16):
             wide = [coherency(channel, group, c, first_row) for c in range(8)]
             for upper in range(2):
                 at = [slice(c * dirs + first_row + 8 * upper, c * dirs + first_row + 8 * upper + 8) for c in range(8)]
-                source = [w[8 * upper : 8 * upper + 8] for w in wide]
-                first = [both[at[c], 0:GROUP] for c in range(8)]
-                propagated = product(first, source)
-                for c in range(8):
-                    propagated_ref[at[c], :] = propagated[c]
-                second = [both[at[c], GROUP : 2 * GROUP] for c in range(8)]
-                model = product_adjoint(propagated, second)
+                source = [with_sum(e) for e in entries([w[8 * upper : 8 * upper + 8] for w in wide])]
+                first = [triple(e) for e in entries([both[at[c], 0:GROUP] for c in range(8)])]
+                propagated = []
+                for row in range(2):
+                    for col in range(2):
+                        value = plain([(source[2 * m + col], first[2 * row + m]) for m in range(2)])
+                        for part in range(2):
+                            propagated_ref[at[2 * (2 * row + col) + part], :] = value[part]
+                        propagated.append(with_sum(value))
+                second = [triple(e) for e in entries([both[at[c], GROUP : 2 * GROUP] for c in range(8)])]
+                model = []
+                for row in range(2):
+                    for col in range(2):
+                        model.extend(conjugated([(propagated[2 * row + n], second[2 * col + n]) for n in range(2)]))
                 total = model if total is None else [t + m for t, m in zip(total, model)]
+                for row in range(2):
+                    for col in range(2):
+                        one, two, three = conjugated([(source[2 * col + n], second[2 * row + n]) for n in range(2)])
+                        turned_ref[at[2 * (2 * row + col)], :] = one + two
+                        turned_ref[at[2 * (2 * row + col) + 1], :] = three - one
         if between[0]:
             between[0]()
         lanes = pl.ds(pl.multiple_of(group * GROUP, GROUP), GROUP)
         residual = []
-        for c in range(8):
-            observed = vis_pad[channel, c : c + 1, lanes]
-            value = (observed - jnp.sum(total[c], axis=0, keepdims=True)) * factor
-            residual.append(jnp.broadcast_to(value, (16, GROUP)))
+        for n in range(4):
+            sums = [jnp.sum(total[3 * n + part], axis=0, keepdims=True) for part in range(3)]
+            pair = (sums[0] + sums[1], sums[0] - sums[2])
+            observed = [vis_pad[channel, 2 * n + part : 2 * n + part + 1, lanes] for part in range(2)]
+            pair = triple([(observed[part] - pair[part]) * factor for part in range(2)])
+            residual.append([jnp.broadcast_to(value, (16, GROUP)) for value in pair])
         place = [slice(n * GROUP, (n + 1) * GROUP) for n in range(4)]
         if following:
             which = [stations_of(side, following[1]) for side in range(2)]
         for first_row in range(0, dirs, 16):
             at = [slice(c * dirs + first_row, c * dirs + first_row + 16) for c in range(8)]
-            source = [coherency(channel, group, c, first_row) for c in range(8)]
-            second = [both[at[c], GROUP : 2 * GROUP] for c in range(8)]
-            conjugated = product_adjoint(second, source)
-            for c, value in enumerate(product_terms(residual, conjugated)):
-                parts[at[c], place[0]], parts[at[c], place[1]] = split(value)
-            propagated = [propagated_ref[at[c], :] for c in range(8)]
-            for c, value in enumerate(adjoint_product_terms(residual, propagated)):
-                parts[at[c], place[2]], parts[at[c], place[3]] = split(value)
+            turned_jones = [with_sum(e) for e in entries([turned_ref[at[c], :] for c in range(8)])]
+            for row in range(2):
+                for col in range(2):
+                    value = plain([(turned_jones[2 * b + col], residual[2 * row + b]) for b in range(2)])
+                    for part in range(2):
+                        where = at[2 * (2 * row + col) + part]
+                        parts[where, place[0]], parts[where, place[1]] = split(value[part])
+            propagated = [with_sum(e) for e in entries([propagated_ref[at[c], :] for c in range(8)])]
+            for row in range(2):
+                for col in range(2):
+                    one, two, three = conjugated([(propagated[2 * a + col], residual[2 * a + row]) for a in range(2)])
+                    for part, value in enumerate((one + two, one - three)):
+                        where = at[2 * (2 * row + col) + part]
+                        parts[where, place[2]], parts[where, place[3]] = split(value)
             if following:
                 fetch(following[0], which, first_row, 16)
             if between[1] and first_row == dirs // 2 - 16:
@@ -222,6 +241,9 @@
         if between[2]:
             between[2]()
 
+    inputs[5].wait()
+    coh_tail[...] = jnp.zeros(coh_tail.shape, BF16)
+    coh_tail[:, :, :, 0 : count - full * GROUP] = coh_ref[:, :, :, full * GROUP : count]
     factors = [counts_ref[channel].astype(F32) * (2.0 * ETA_STEP / SAMPLES) for channel in range(own)]
 
     def step(_, carry):
@@ -245,7 +267,8 @@
         last = groups - 1
         visit(0, last, factors[0], (1, last))
         scatter(1, last - 1)
-        visit(1, last, factors[1])
+        turn(0)
+        visit(1, last, factors[1], None, [None, lambda: turn(1), None])
         scatter(0, last)
         scatter(1, last)
         for channel in range(own):
@@ -279,10 +302,11 @@
     inverse = [[float(v) for v in row] for row in gram_inverse(channels).astype(np.float32)]
     vmem = pl.BlockSpec(memory_space=pltpu.VMEM)
     smem = pl.BlockSpec(memory_space=pltpu.SMEM)
+    anywhere = pl.BlockSpec(memory_space=pl.ANY)
     return pl.pallas_call(
         functools.partial(descend_kernel, channels, blocks, inverse),
         out_shape=tuple(jax.ShapeDtypeStruct(a.shape, F32) for a in (jones, duals, consensus)),
-        in_specs=[vmem, smem, vmem, vmem, vmem, vmem, vmem],
+        in_specs=[anywhere, smem] + [anywhere] * 5,
         out_specs=(vmem, vmem, vmem),
         scratch_shapes=[
             pltpu.VMEM((stations // 2 + 1,) + unit, F32),
@@ -292,19 +316,22 @@
             pltpu.VMEM((groups, GROUP, 4 * GROUP), BF16),
             pltpu.VMEM((own, 8, dirs, GROUP), F32),
             pltpu.VMEM((own, 8, dirs, GROUP), F32),
-            pltpu.VMEM((stations, 8, dirs), F32),
+            pltpu.VMEM((own, stations, 8, dirs), F32),
             [pltpu.VMEM((rows, 2 * GROUP), F32)] * own,
+            [pltpu.VMEM((rows, GROUP), F32)] * own,
             [pltpu.VMEM((rows, GROUP), F32)] * own,
             [pltpu.VMEM((rows, 4 * GROUP), BF16)] * own,
             [pltpu.VMEM((rows, GROUP), F32)] * own,
         ]
+        + [pltpu.VMEM(a.shape, a.dtype) for a in (pairs, jones, duals, consensus, visibilities, coherencies)]
+        + [dma((6,))]
         + [pltpu.VMEM((planes,) + unit, F32)] * 3
         + [pltpu.VMEM((SIDE,) + unit, F32), pltpu.VMEM((2 * planes,) + unit, F32)]
         + [dma((planes,))] * 4
         + [dma((SIDE,))] * 2
         + [dma((planes,))] * 4,
         compiler_params=pltpu.CompilerParams(
-            collective_id=0, has_side_effects=True, vmem_limit_bytes=28 * 2**20
+            collective_id=0, has_side_effects=True, vmem_limit_bytes=56 * 2**20
         ),
         name="descend",
     )(pairs, counts, jones, duals, consensus, visibilities, coherencies)
@@ -364,18 +391,33 @@
         unit = core * 16 + back(dx, dy)
         c = rc(full.at[unit], full.at[unit], s5.at[n], r5.at[n], dev(u, other))
         c.start(); c5.append(c)
-    for c in c5: c.wait_recv()
-    for c in c1 + c2 + c3 + c4 + c5: c.wait_send()
     own, stations, _, dirs = jones_ref.shape
     near = stations // 2
-    for i in range(3):
-        consensus_out[i, 0:near] = full[0:near, i, :, 0:dirs]
-        consensus_out[i, near : 2 * near] = full[0:near, i, :, dirs : 2 * dirs]
     offset = (z * blocks + chan) * own
-    for channel in range(own):
-        basis = bernstein(((offset + channel).astype(F32) + 0.5) * (1.0 / channels))
-        smooth = sum(basis[i] * consensus_out[i] for i in range(3))
-        duals_out[channel] = duals_ref[channel] + RHO_PENALTY * (jones_ref[channel] - smooth)
+    basis = [bernstein(((offset + channel).astype(F32) + 0.5) * (1.0 / channels)) for channel in range(own)]
+
+    def finish(unit):
+        @pl.when(unit < near)
+        def _():
+            for side in range(2):
+                station = unit + side * near
+                agreed = [full[unit, i, :, side * dirs : (side + 1) * dirs] for i in range(3)]
+                for i in range(3):
+                    consensus_out[i, station] = agreed[i]
+                for channel in range(own):
+                    smooth = sum(basis[channel][i] * agreed[i] for i in range(3))
+                    duals_out[channel, station] = duals_ref[channel, station] + RHO_PENALTY * (
+                        jones_ref[channel, station] - smooth
+                    )
+
+    finish(mine)
+    for dx, dy in reversed(steps):
+        finish(core * 16 + back(dx, dy))
+    for n, c in enumerate(c5):
+        c.wait_recv()
+        dx, dy = ([(0, 0)] + list(reversed(steps)))[n]
+        finish(other * 16 + back(dx, dy))
+    for c in c1 + c2 + c3 + c4 + c5: c.wait_send()
 
 
 def shards(jones_start, duals_start, consensus_start, visibilities, coherencies, pairs, counts):

time: 65.8 us -> 64.3 us (0.977)
  local copies, waits for them, and re-layouts: 10 us -> 5.75 us
  Pallas kernels: 54.8 us -> 57.6 us
    unnamed x17 -> x3, local copies, waits for them, and re-layouts: 10 us -> 5.75 us
    pallas_call x1, Pallas kernels: 54.8 us -> 57.6 us  [descend(): pl.pallas_call(functools.partial(descend_kernel, channels, blocks, invers...]
where the time goes in v4:
time: 64.3 us; the launch traced here: 64 us
  Pallas kernels  57.6 us (90%)
  local copies, waits for them, and re-layouts  5.75 us (9%)
    pallas_call x1, Pallas kernels, descend(): pl.pallas_call(functools.partial(descend_kernel, channels, blocks, invers...  57.6 us
    unnamed x3, local copies, waits for them, and re-layouts  5.75 us

profile of v4, /device:TPU:1, one launch (start us, length us, event | category | flops | bytes accessed | tf_op | source)
XLA Modules:
  0.0 64.0 jit_solution(15680632584265663864)
XLA Ops:
  0.6 57.6 %descend.1 = (f32[2,62,8,64]{3,2,1,0:T(8,128)}, f32[2,62,8,64]{3,2,1,0:T(8,128)}, f32[3,62,8,64]{3,2,1,0:T(8,128)}) custom-call(s32[2,1891]{1,0:T(2,128)} %pairs_in.1, s32[2]{0:T(128)} %counts_ref.1, f32[2,62,8,64]{3,2,1,0:T(8,128)} %bitcast.10, f32[2,62,8,64]{3,2,1,0:T(8,128)} %bitcast.11, f32[3,62,8,64]{3,2,1,0:T(8,128)} %bitcast.7, f32[2,8,1891]{2,1,0:T(8,128)} %vis_in.1, ...), custom_call_target="tpu_custom_call" | custom-call | tf_op jit(solution)/shard_map/descend/pallas_call | solution.py:306
  58.3 1.9 %copy.13 = f32[2,8,64,62]{2,1,3,0:T(8,128)} copy(f32[2,8,64,62]{2,1,3,0:T(8,128)} %bitcast.9) | data formatting | bytes 507904
  60.1 1.9 %copy.14 = f32[2,8,64,62]{2,1,3,0:T(8,128)} copy(f32[2,8,64,62]{2,1,3,0:T(8,128)} %bitcast.8) | data formatting | bytes 507904
  62.0 2.0 %copy.15 = f32[3,8,64,62]{2,1,3,0:T(8,128)} copy(f32[3,8,64,62]{2,1,3,0:T(8,128)} %bitcast.6) | data formatting | bytes 761856

commit v5 on v4

--- a/solution.py
+++ b/solution.py
@@ -105,9 +105,11 @@
 
     greet(False)
     inputs = [
-        (pairs_in, pairs_ref), (vis_in, vis_ref), (consensus_in, consensus_ref), (duals_in, duals_ref),
-        (jones_in, jones_ref), (coh_in, coh_ref),
+        (pairs_in, pairs_ref), (jones_in, jones_ref), (vis_in, vis_ref), (consensus_in, consensus_ref),
+        (duals_in, duals_ref),
     ]
+    for channel in range(own):
+        inputs.extend((coh_in.at[channel, c], coh_ref.at[channel, c]) for c in range(8))
     inputs = [pltpu.make_async_copy(a, b, arrived.at[n]) for n, (a, b) in enumerate(inputs)]
     for copy in inputs:
         copy.start()
@@ -125,10 +127,10 @@
                 where = (2 * side + part) * GROUP
                 spread_hot[group, :, where : where + GROUP] = hot
 
-    inputs[1].wait()
+    inputs[2].wait()
     vis_pad[...] = jnp.zeros(vis_pad.shape, F32)
     vis_pad[:, :, 0:count] = vis_ref[...]
-    for copy in inputs[2:5]:
+    for copy in (inputs[1], inputs[3], inputs[4]):
         copy.wait()
 
     basis = []
@@ -241,7 +243,8 @@
         if between[2]:
             between[2]()
 
-    inputs[5].wait()
+    for copy in inputs[5:]:
+        copy.wait()
     coh_tail[...] = jnp.zeros(coh_tail.shape, BF16)
     coh_tail[:, :, :, 0 : count - full * GROUP] = coh_ref[:, :, :, full * GROUP : count]
     factors = [counts_ref[channel].astype(F32) * (2.0 * ETA_STEP / SAMPLES) for channel in range(own)]
@@ -305,7 +308,7 @@
     anywhere = pl.BlockSpec(memory_space=pl.ANY)
     return pl.pallas_call(
         functools.partial(descend_kernel, channels, blocks, inverse),
-        out_shape=tuple(jax.ShapeDtypeStruct(a.shape, F32) for a in (jones, duals, consensus)),
+        out_shape=tuple(pltpu.VMEM(a.shape, F32) for a in (jones, duals, consensus)),
         in_specs=[anywhere, smem] + [anywhere] * 5,
         out_specs=(vmem, vmem, vmem),
         scratch_shapes=[
@@ -324,7 +327,7 @@
             [pltpu.VMEM((rows, GROUP), F32)] * own,
         ]
         + [pltpu.VMEM(a.shape, a.dtype) for a in (pairs, jones, duals, consensus, visibilities, coherencies)]
-        + [dma((6,))]
+        + [dma((5 + 8 * own,))]
         + [pltpu.VMEM((planes,) + unit, F32)] * 3
         + [pltpu.VMEM((SIDE,) + unit, F32), pltpu.VMEM((2 * planes,) + unit, F32)]
         + [dma((planes,))] * 4
@@ -420,12 +423,33 @@
     for c in c1 + c2 + c3 + c4 + c5: c.wait_send()
 
 
+def deliver_kernel(*refs):
+    half = len(refs) // 2
+    copies = [pltpu.make_async_copy(refs[n], refs[half + n], refs[-1].at[n]) for n in range(half)]
+    for copy in copies:
+        copy.start()
+    for copy in copies:
+        copy.wait()
+
+
+def deliver(arrays):
+    return pl.pallas_call(
+        deliver_kernel,
+        out_shape=tuple(jax.ShapeDtypeStruct(a.shape, a.dtype) for a in arrays),
+        in_specs=[pl.BlockSpec(memory_space=pltpu.VMEM)] * len(arrays),
+        out_specs=tuple(pl.BlockSpec(memory_space=pl.ANY) for _ in arrays),
+        scratch_shapes=[pltpu.SemaphoreType.DMA((len(arrays),))],
+        compiler_params=pltpu.CompilerParams(vmem_limit_bytes=2**20),
+        name="deliver",
+    )(*arrays)
+
+
 def shards(jones_start, duals_start, consensus_start, visibilities, coherencies, pairs, counts):
     blocks = lax.axis_size("chan")
     channels = jones_start.shape[0] * lax.axis_size("grp") * blocks
     jones, duals, consensus = (jnp.transpose(a, (0, 3, 1, 2)) for a in (jones_start, duals_start, consensus_start))
     outs = descend(channels, blocks, pairs, counts, jones, duals, consensus, visibilities, coherencies)
-    return tuple(jnp.transpose(a, (0, 2, 3, 1)) for a in outs)
+    return tuple(jnp.transpose(a, (0, 2, 3, 1)) for a in deliver(outs))
 
 
 def solution(mesh):

time: 64.3 us -> 58.6 us (0.911)
  local copies, waits for them, and re-layouts: 5.75 us -> 0 us
    unnamed x3 -> x0, local copies, waits for them, and re-layouts: 5.75 us -> none
    pallas_call x0 -> x1, Pallas kernels: none -> 1.23 us  [deliver(): pl.pallas_call(deliver_kernel, out_shape=tuple((jax.ShapeDtypeStruct(a.sh...]
    pallas_call x1, Pallas kernels: 57.6 us -> 56.6 us  [descend(): pl.pallas_call(functools.partial(descend_kernel, channels, blocks, invers...]
where the time goes in v5:
time: 58.6 us; the launch traced here: 58.5 us
  Pallas kernels  57.8 us (99%)
  between operations  0.64 us (1%)
    pallas_call x1, Pallas kernels, descend(): pl.pallas_call(functools.partial(descend_kernel, channels, blocks, invers...  56.6 us
    pallas_call x1, Pallas kernels, deliver(): pl.pallas_call(deliver_kernel, out_shape=tuple((jax.ShapeDtypeStruct(a.sh...  1.23 us

profile of v5, /device:TPU:1, one launch (start us, length us, event | category | flops | bytes accessed | tf_op | source)
XLA Modules:
  0.0 58.5 jit_solution(14793979576580798549)
XLA Ops:
  0.6 56.6 %descend.1 = (f32[2,62,8,64]{3,2,1,0:T(8,128)S(1)}, f32[2,62,8,64]{3,2,1,0:T(8,128)S(1)}, f32[3,62,8,64]{3,2,1,0:T(8,128)S(1)}) custom-call(s32[2,1891]{1,0:T(2,128)} %pairs_in.1, s32[2]{0:T(128)} %counts_ref.1, f32[2,62,8,64]{3,2,1,0:T(8,128)} %bitcast.7, f32[2,62,8,64]{3,2,1,0:T(8,128)} %bitcast.8, f32[3,62,8,64]{3,2,1,0:T(8,128)} %bitcast.6, ...), custom_call_target="tpu_custom_call" | custom-call | tf_op jit(solution)/shard_map/descend/pallas_call | solution.py:309
  57.2 1.2 %deliver.1 = (f32[2,62,8,64]{3,2,1,0:T(8,128)}, f32[2,62,8,64]{3,2,1,0:T(8,128)}, f32[3,62,8,64]{3,2,1,0:T(8,128)}) custom-call(f32[2,62,8,64]{3,2,1,0:T(8,128)S(1)} %get-tuple-element.9.refs_0_, f32[2,62,8,64]{3,2,1,0:T(8,128)S(1)} %get-tuple-element.10.refs_1_, f32[3,62,8,64]{3,2,1,0:T(8,128)S(1)} %get-tuple-element.11.refs_2_), custom_call_target="tpu_custom_call" | custom-call | tf_op jit(solution)/shard_map/deliver/pallas_call | solution.py:436

commit v6 on v5

--- a/solution.py
+++ b/solution.py
@@ -17,6 +17,7 @@
 BF16 = jnp.bfloat16
 MESH = pl.DeviceIdType.MESH
 SIDE = 4
+FAR = 5
 
 
 def bernstein(position):
@@ -70,21 +71,26 @@
     return high, low
 
 
+def offsets():
+    near = [min(n, SIDE - n) for n in range(SIDE)]
+    pairs = [(dx, dy) for dx in range(SIDE) for dy in range(SIDE) if dx or dy]
+    return sorted(pairs, key=lambda pair: -(near[pair[0]] + near[pair[1]]))
+
+
 def greet(wait):
     barrier = pltpu.get_barrier_semaphore()
     z, chan = lax.axis_index("grp"), lax.axis_index("chan")
     core, u = chan % 2, chan // 2
     if wait:
-        pl.semaphore_wait(barrier, 1 + SIDE * SIDE - 1 + SIDE - 1)
+        pl.semaphore_wait(barrier, 1 + SIDE * SIDE - 1 + SIDE - 1 + FAR)
         return
     pl.semaphore_signal(barrier, inc=1, device_id={"grp": z, "chan": u * 2 + 1 - core}, device_id_type=MESH)
-    for dx in range(SIDE):
-        for dy in range(SIDE):
-            if dx or dy:
-                there = ((u // SIDE + dx) % SIDE) * SIDE + (u % SIDE + dy) % SIDE
-                pl.semaphore_signal(
-                    barrier, inc=1, device_id={"grp": z, "chan": there * 2 + core}, device_id_type=MESH
-                )
+    for n, (dx, dy) in enumerate(offsets()):
+        there = ((u // SIDE + dx) % SIDE) * SIDE + (u % SIDE + dy) % SIDE
+        for side in (core, 1 - core) if n < FAR else (core,):
+            pl.semaphore_signal(
+                barrier, inc=1, device_id={"grp": z, "chan": there * 2 + side}, device_id_type=MESH
+            )
     for dz in range(1, SIDE):
         pl.semaphore_signal(barrier, inc=1, device_id={"grp": (z + dz) % SIDE, "chan": chan}, device_id_type=MESH)
 
@@ -329,10 +335,12 @@
         + [pltpu.VMEM(a.shape, a.dtype) for a in (pairs, jones, duals, consensus, visibilities, coherencies)]
         + [dma((5 + 8 * own,))]
         + [pltpu.VMEM((planes,) + unit, F32)] * 3
+        + [pltpu.VMEM((FAR,) + unit, F32)]
         + [pltpu.VMEM((SIDE,) + unit, F32), pltpu.VMEM((2 * planes,) + unit, F32)]
         + [dma((planes,))] * 4
         + [dma((SIDE,))] * 2
-        + [dma((planes,))] * 4,
+        + [dma((planes,))] * 4
+        + [dma((FAR,))] * 4,
         compiler_params=pltpu.CompilerParams(
             collective_id=0, has_side_effects=True, vmem_limit_bytes=56 * 2**20
         ),
@@ -342,58 +350,73 @@
 
 def agree_kernel(
     channels, blocks, inverse, s_ref, jones_ref, duals_ref, consensus_out, duals_out,
-    recv_core, mid, recv_plane, recv_col, full, s1, r1, s2, r2, s3, r3, s4, r4, s5, r5,
+    recv_core, mid, recv_plane, recv_far, recv_col, full, s1, r1, s2, r2, s3, r3, s4, r4, s5, r5, s6, r6, s7, r7,
 ):
     z = lax.axis_index("grp"); chan = lax.axis_index("chan")
     core = chan % 2; u = chan // 2; x = u // SIDE; y = u % SIDE
     other = 1 - core
     def peer(dx, dy):
         return ((x + dx) % SIDE) * SIDE + (y + dy) % SIDE
-    steps = sorted([(dx, dy) for dx in range(SIDE) for dy in range(SIDE) if dx or dy], key=lambda s: -(min(s[0],4-s[0])+min(s[1],4-s[1])))
+    steps = offsets()
     def back(dx, dy):
         return ((x - dx + SIDE) % SIDE) * SIDE + (y - dy + SIDE) % SIDE
     def dev(uu, cc): return {"grp": z, "chan": uu * 2 + cc}
     greet(True)
     order = steps + [(0, 0)]
-    def rc(src, dst, ss, rs, d):
-        return pltpu.make_async_remote_copy(src_ref=src, dst_ref=dst, send_sem=ss, recv_sem=rs, device_id=d, device_id_type=MESH)
-    c1 = []
+    last = len(steps)
+
+    def send(source, target, sent, received, device):
+        copy = pltpu.make_async_remote_copy(
+            src_ref=source, dst_ref=target, send_sem=sent, recv_sem=received, device_id=device, device_id_type=MESH
+        )
+        copy.start()
+        return copy
+
+    c2, c6 = {}, {}
+    for n, (dx, dy) in enumerate(order[:FAR]):
+        there = peer(dx, dy)
+        c2[n] = send(s_ref.at[core * 16 + there], recv_plane.at[n], s2.at[n], r2.at[n], dev(there, core))
+        c6[n] = send(s_ref.at[other * 16 + there], recv_far.at[n], s6.at[n], r6.at[n], dev(there, other))
+    c1 = {}
     for n, (dx, dy) in enumerate(order):
-        c = rc(s_ref.at[other * 16 + peer(dx, dy)], recv_core.at[n], s1.at[n], r1.at[n], dev(u, other))
-        c.start(); c1.append(c)
-    c2 = []
+        if n >= FAR:
+            c1[n] = send(s_ref.at[other * 16 + peer(dx, dy)], recv_core.at[n], s1.at[n], r1.at[n], dev(u, other))
     for n, (dx, dy) in enumerate(order):
-        c1[n].wait_recv()
-        mid[n] = s_ref[core * 16 + peer(dx, dy)] + recv_core[n]
-        if n < 15:
-            c = rc(mid.at[n], recv_plane.at[n], s2.at[n], r2.at[n], dev(peer(dx, dy), core))
-            c.start(); c2.append(c)
-    total = mid[15]
-    for n in range(15):
+        if n >= FAR:
+            c1[n].wait_recv()
+            mid[n] = s_ref[core * 16 + peer(dx, dy)] + recv_core[n]
+            if n < last:
+                c2[n] = send(mid.at[n], recv_plane.at[n], s2.at[n], r2.at[n], dev(peer(dx, dy), core))
+    total = mid[last]
+    for n in reversed(range(last)):
         c2[n].wait_recv()
         total = total + recv_plane[n]
+        if n < FAR:
+            c6[n].wait_recv()
+            total = total + recv_far[n]
     recv_col[z] = total
-    c3 = []
-    for dz in range(1, SIDE):
-        c = rc(recv_col.at[z], recv_col.at[z], s3.at[dz], r3.at[dz], {"grp": (z + dz) % SIDE, "chan": chan})
-        c.start(); c3.append(c)
-    for c in c3: c.wait_recv()
+    c3 = [
+        send(recv_col.at[z], recv_col.at[z], s3.at[dz], r3.at[dz], {"grp": (z + dz) % SIDE, "chan": chan})
+        for dz in range(1, SIDE)
+    ]
+    for copy in c3:
+        copy.wait_recv()
     total = recv_col[0] + recv_col[1] + recv_col[2] + recv_col[3]
     mine = core * 16 + u
     for i in range(3):
         full[mine, i] = sum(inverse[i][j] * total[j] for j in range(3))
-    c4 = []
+    c4, c5, c7 = {}, {}, {}
     for n, (dx, dy) in enumerate(steps):
-        c = rc(full.at[mine], full.at[mine], s4.at[n], r4.at[n], dev(peer(dx, dy), core))
-        c.start(); c4.append(c)
-    c5 = []
-    c = rc(full.at[mine], full.at[mine], s5.at[15], r5.at[15], dev(u, other))
-    c.start(); c5.append(c)
-    for n, (dx, dy) in reversed(list(enumerate(steps))):
+        there = peer(dx, dy)
+        c4[n] = send(full.at[mine], full.at[mine], s4.at[n], r4.at[n], dev(there, core))
+        if n < FAR:
+            c7[n] = send(full.at[mine], full.at[mine], s7.at[n], r7.at[n], dev(there, other))
+    c5[last] = send(full.at[mine], full.at[mine], s5.at[last], r5.at[last], dev(u, other))
+    for n in reversed(range(last)):
         c4[n].wait_recv()
-        unit = core * 16 + back(dx, dy)
-        c = rc(full.at[unit], full.at[unit], s5.at[n], r5.at[n], dev(u, other))
-        c.start(); c5.append(c)
+        if n >= FAR:
+            unit = core * 16 + back(*steps[n])
+            c5[n] = send(full.at[unit], full.at[unit], s5.at[n], r5.at[n], dev(u, other))
     own, stations, _, dirs = jones_ref.shape
     near = stations // 2
     offset = (z * blocks + chan) * own
@@ -414,13 +437,19 @@
                     )
 
     finish(mine)
-    for dx, dy in reversed(steps):
-        finish(core * 16 + back(dx, dy))
-    for n, c in enumerate(c5):
-        c.wait_recv()
-        dx, dy = ([(0, 0)] + list(reversed(steps)))[n]
-        finish(other * 16 + back(dx, dy))
-    for c in c1 + c2 + c3 + c4 + c5: c.wait_send()
+    for n in reversed(range(last)):
+        finish(core * 16 + back(*steps[n]))
+    for n in reversed(range(FAR, last + 1)):
+        c5[n].wait_recv()
+        finish(other * 16 + back(*order[n]))
+    for n in range(FAR):
+        c7[n].wait_recv()
+        finish(other * 16 + back(*steps[n]))
+    for copies in (c1, c2, c4, c5, c6, c7):
+        for copy in copies.values():
+            copy.wait_send()
+    for copy in c3:
+        copy.wait_send()
 
 
 def deliver_kernel(*refs):

time: 58.6 us -> 59.8 us (1.020)
  Pallas kernels: 57.8 us -> 59 us
    pallas_call x1, Pallas kernels: 56.6 us -> 57.7 us  [descend(): pl.pallas_call(functools.partial(descend_kernel, channels, blocks, invers...]
where the time goes in v6:
time: 59.8 us; the launch traced here: 59.6 us
  Pallas kernels  59 us (99%)
  between operations  0.64 us (1%)
    pallas_call x1, Pallas kernels, descend(): pl.pallas_call(functools.partial(descend_kernel, channels, blocks, invers...  57.7 us
    pallas_call x1, Pallas kernels, deliver(): pl.pallas_call(deliver_kernel, out_shape=tuple((jax.ShapeDtypeStruct(a.sh...  1.23 us

profile of v6, /device:TPU:1, one launch (start us, length us, event | category | flops | bytes accessed | tf_op | source)
XLA Modules:
  0.0 59.6 jit_solution(8560548699073488849)
XLA Ops:
  0.6 57.7 %descend.1 = (f32[2,62,8,64]{3,2,1,0:T(8,128)S(1)}, f32[2,62,8,64]{3,2,1,0:T(8,128)S(1)}, f32[3,62,8,64]{3,2,1,0:T(8,128)S(1)}) custom-call(s32[2,1891]{1,0:T(2,128)} %pairs_in.1, s32[2]{0:T(128)} %counts_ref.1, f32[2,62,8,64]{3,2,1,0:T(8,128)} %bitcast.7, f32[2,62,8,64]{3,2,1,0:T(8,128)} %bitcast.8, f32[3,62,8,64]{3,2,1,0:T(8,128)} %bitcast.6, ...), custom_call_target="tpu_custom_call" | custom-call | tf_op jit(solution)/shard_map/descend/pallas_call | solution.py:315
  58.4 1.2 %deliver.1 = (f32[2,62,8,64]{3,2,1,0:T(8,128)}, f32[2,62,8,64]{3,2,1,0:T(8,128)}, f32[3,62,8,64]{3,2,1,0:T(8,128)}) custom-call(f32[2,62,8,64]{3,2,1,0:T(8,128)S(1)} %get-tuple-element.9.refs_0_, f32[2,62,8,64]{3,2,1,0:T(8,128)S(1)} %get-tuple-element.10.refs_1_, f32[3,62,8,64]{3,2,1,0:T(8,128)S(1)} %get-tuple-element.11.refs_2_), custom_call_target="tpu_custom_call" | custom-call | tf_op jit(solution)/shard_map/deliver/pallas_call | solution.py:465

commit v7 on v5

--- a/solution.py
+++ b/solution.py
@@ -169,11 +169,11 @@
         lanes = pl.ds(group * GROUP if isinstance(group, int) else pl.multiple_of(group * GROUP, GROUP), GROUP)
         return jnp.broadcast_to(jnp.maximum(pairs_pad[side : side + 1, lanes], 0), (8, GROUP))
 
-    def fetch(channel, which, first_row, depth):
+    def fetch(channel, which, first_row, depth, sides=(0, 1)):
         for row in range(first_row, first_row + depth, 8):
             for c in range(8):
                 table = jones_cur[channel, c, row : row + 8, :]
-                for side in range(2):
+                for side in sides:
                     both_now[channel][c * dirs + row : c * dirs + row + 8, side * GROUP : (side + 1) * GROUP] = (
                         jnp.take_along_axis(table, which[side], axis=1)
                     )
@@ -183,7 +183,11 @@
         parts = grad_parts[channel]
         lanes = pl.ds(group * GROUP if isinstance(group, int) else pl.multiple_of(group * GROUP, GROUP), GROUP)
         total = None
+        if following:
+            which = [stations_of(side, following[1]) for side in range(2)]
         for first_row in range(0, dirs, 16):
+            if following and first_row < 32:
+                fetch(following[0], which, first_row, 16, (0,))
             wide = [coherency(channel, group, c, first_row) for c in range(8)]
             for upper in range(2):
                 at = [slice(c * dirs + first_row + 8 * upper, c * dirs + first_row + 8 * upper + 8) for c in range(8)]
@@ -237,7 +241,7 @@
                         where = at[2 * (2 * row + col) + part]
                         parts[where, place[2]], parts[where, place[3]] = split(value)
             if following:
-                fetch(following[0], which, first_row, 16)
+                fetch(following[0], which, first_row, 16, (0, 1) if first_row >= 32 else (1,))
             if between[1] and first_row == dirs // 2 - 16:
                 between[1]()
         if between[2]:

time: 58.6 us -> 58.2 us (level)
  no operation moved by 1% of the time
where the time goes in v7:
time: 58.2 us; the launch traced here: 58.1 us
  Pallas kernels  57.4 us (99%)
  between operations  0.64 us (1%)
    pallas_call x1, Pallas kernels, descend(): pl.pallas_call(functools.partial(descend_kernel, channels, blocks, invers...  56.2 us
    pallas_call x1, Pallas kernels, deliver(): pl.pallas_call(deliver_kernel, out_shape=tuple((jax.ShapeDtypeStruct(a.sh...  1.23 us

profile of v7, /device:TPU:1, one launch (start us, length us, event | category | flops | bytes accessed | tf_op | source)
XLA Modules:
  0.0 58.1 jit_solution(13458487045346799210)
XLA Ops:
  0.6 56.2 %descend.1 = (f32[2,62,8,64]{3,2,1,0:T(8,128)S(1)}, f32[2,62,8,64]{3,2,1,0:T(8,128)S(1)}, f32[3,62,8,64]{3,2,1,0:T(8,128)S(1)}) custom-call(s32[2,1891]{1,0:T(2,128)} %pairs_in.1, s32[2]{0:T(128)} %counts_ref.1, f32[2,62,8,64]{3,2,1,0:T(8,128)} %bitcast.7, f32[2,62,8,64]{3,2,1,0:T(8,128)} %bitcast.8, f32[3,62,8,64]{3,2,1,0:T(8,128)} %bitcast.6, ...), custom_call_target="tpu_custom_call" | custom-call | tf_op jit(solution)/shard_map/descend/pallas_call | solution.py:313
  56.8 1.2 %deliver.1 = (f32[2,62,8,64]{3,2,1,0:T(8,128)}, f32[2,62,8,64]{3,2,1,0:T(8,128)}, f32[3,62,8,64]{3,2,1,0:T(8,128)}) custom-call(f32[2,62,8,64]{3,2,1,0:T(8,128)S(1)} %get-tuple-element.9.refs_0_, f32[2,62,8,64]{3,2,1,0:T(8,128)S(1)} %get-tuple-element.10.refs_1_, f32[3,62,8,64]{3,2,1,0:T(8,128)S(1)} %get-tuple-element.11.refs_2_), custom_call_target="tpu_custom_call" | custom-call | tf_op jit(solution)/shard_map/deliver/pallas_call | solution.py:440

commit v8 on v7

--- a/solution.py
+++ b/solution.py
@@ -226,6 +226,8 @@
             which = [stations_of(side, following[1]) for side in range(2)]
         for first_row in range(0, dirs, 16):
             at = [slice(c * dirs + first_row, c * dirs + first_row + 16) for c in range(8)]
+            if following:
+                fetch(following[0], which, first_row, 16, (0, 1) if first_row >= 32 else (1,))
             turned_jones = [with_sum(e) for e in entries([turned_ref[at[c], :] for c in range(8)])]
             for row in range(2):
                 for col in range(2):
@@ -240,8 +242,6 @@
                     for part, value in enumerate((one + two, one - three)):
                         where = at[2 * (2 * row + col) + part]
                         parts[where, place[2]], parts[where, place[3]] = split(value)
-            if following:
-                fetch(following[0], which, first_row, 16, (0, 1) if first_row >= 32 else (1,))
             if between[1] and first_row == dirs // 2 - 16:
                 between[1]()
         if between[2]:

time: 58.2 us -> 58.2 us (level)
  no operation moved by 1% of the time
where the time goes in v8:
time: 58.2 us; the launch traced here: 58.1 us
  Pallas kernels  57.4 us (99%)
  between operations  0.64 us (1%)
    pallas_call x1, Pallas kernels, descend(): pl.pallas_call(functools.partial(descend_kernel, channels, blocks, invers...  56.2 us
    pallas_call x1, Pallas kernels, deliver(): pl.pallas_call(deliver_kernel, out_shape=tuple((jax.ShapeDtypeStruct(a.sh...  1.23 us

profile of v8, /device:TPU:1, one launch (start us, length us, event | category | flops | bytes accessed | tf_op | source)
XLA Modules:
  0.0 58.1 jit_solution(13458487045346799210)
XLA Ops:
  0.6 56.2 %descend.1 = (f32[2,62,8,64]{3,2,1,0:T(8,128)S(1)}, f32[2,62,8,64]{3,2,1,0:T(8,128)S(1)}, f32[3,62,8,64]{3,2,1,0:T(8,128)S(1)}) custom-call(s32[2,1891]{1,0:T(2,128)} %pairs_in.1, s32[2]{0:T(128)} %counts_ref.1, f32[2,62,8,64]{3,2,1,0:T(8,128)} %bitcast.7, f32[2,62,8,64]{3,2,1,0:T(8,128)} %bitcast.8, f32[3,62,8,64]{3,2,1,0:T(8,128)} %bitcast.6, ...), custom_call_target="tpu_custom_call" | custom-call | tf_op jit(solution)/shard_map/descend/pallas_call | solution.py:313
  56.8 1.2 %deliver.1 = (f32[2,62,8,64]{3,2,1,0:T(8,128)}, f32[2,62,8,64]{3,2,1,0:T(8,128)}, f32[3,62,8,64]{3,2,1,0:T(8,128)}) custom-call(f32[2,62,8,64]{3,2,1,0:T(8,128)S(1)} %get-tuple-element.9.refs_0_, f32[2,62,8,64]{3,2,1,0:T(8,128)S(1)} %get-tuple-element.10.refs_1_, f32[3,62,8,64]{3,2,1,0:T(8,128)S(1)} %get-tuple-element.11.refs_2_), custom_call_target="tpu_custom_call" | custom-call | tf_op jit(solution)/shard_map/deliver/pallas_call | solution.py:440
